TPU v7x, 256 devices: a whole 4x4x8 slice. The times are simulated.
256 devices in a mesh: dom: 64 (over z, y, core), space: 4 (over x).
Axes of the slice: x: 4, y: 4, z: 8, core: 2. Of those that a mesh axis runs over, the one named last changes fastest.
Arguments:
- ensemble: float32 [64, 2, 32, 4096], P('dom', None, 'space'), may hold values from -6 to 6
- offspring: int32 [64], replicated, may hold values from 0 to 16, as said below
- new_owner: int32 [64], replicated, may hold values from 0 to 63, as said below
- perturb: bfloat16 [64, 2, 2, 32, 4096], P('dom', None, None, 'space'), may hold values from -6 to 6
- observed: float32 [32, 4096], P('space'), may hold values from -6 to 6
- nudge_rate: float32 [32], P('space'), may hold values from 1 to 10
Outputs:
- analysis: float32 [64, 2, 32, 4096], P('dom', None, 'space')
Inputs may be any that keep to these rules, and one draw needn't show every extreme that they name: The counts sum to 64; at most 4 particles have more than one offspring. A permutation. Copies are listed parent by parent in increasing order of the parent; copy j becomes member new_owner[j], and the first copy of every particle with offspring becomes that particle's own member.
All inputs are finite; a program needn't handle non-finite values.
Results may differ from a plain program's by a relative error of at most 0.0003.
Values sent between devices are 32-bit elements; how exact they have to be, the bound alone decides.
A program may use at most 64 MiB of HBM per device.

v0:
```python
import jax
import jax.numpy as jnp
from jax import lax
from jax.sharding import PartitionSpec as P

STEPS = 2
SWEEPS = 2


time_step = 0.05
beta_plane = 1.0
noise_scale = 0.5


def with_halo(block, sides, width):
    for axis, dim in sides:
        count = lax.axis_size(axis)
        forward = [(i, i + 1) for i in range(count - 1)]
        backward = [(target, source) for source, target in forward]
        low = lax.ppermute(
            lax.slice_in_dim(block, block.shape[dim] - width, None, axis=dim), axis, forward
        )
        high = lax.ppermute(lax.slice_in_dim(block, 0, width, axis=dim), axis, backward)
        block = jnp.concatenate([low, block, high], axis=dim)
    return block


def layer_coupling():
    return jnp.array([0.4, 0.6], dtype=jnp.float32)[:, None, None]


def bottom_drag():
    return jnp.array([0.0, 0.2], dtype=jnp.float32)[:, None, None]


def laplace_rim(values):
    centre = values[:, 1:-1]
    return (
        values[:, 2:]
        + values[:, :-2]
        + jnp.roll(centre, 1, 2)
        + jnp.roll(centre, -1, 2)
        - 4.0 * centre
    )


def coupling(values):
    return layer_coupling() * (values[::-1] - values)


def model_step(stream, perturb_now, observed, nudge_rate):
    row_count = stream.shape[1]
    extended = with_halo(stream, (("space", 1),), 2)
    middle = extended[:, 1:-1]
    potential_rim = laplace_rim(extended) + coupling(middle)
    global_row = (
        lax.axis_index("space") * row_count + jnp.arange(row_count + 2, dtype=jnp.int32) - 1
    )
    inside = (global_row >= 0) & (global_row < row_count * lax.axis_size("space"))
    potential_rim = jnp.where(inside[None, :, None], potential_rim, 0.0)
    potential = potential_rim[:, 1:-1]
    east_stream = jnp.roll(stream, -1, 2) - jnp.roll(stream, 1, 2)
    north_stream = middle[:, 2:] - middle[:, :-2]
    east_pot = jnp.roll(potential, -1, 2) - jnp.roll(potential, 1, 2)
    north_pot = potential_rim[:, 2:] - potential_rim[:, :-2]
    advection = (east_stream * north_pot - north_stream * east_pot) / 4.0
    tendency = -advection - beta_plane * 0.5 * east_stream - bottom_drag() * potential
    upper = time_step * nudge_rate[:, None] * (observed - stream[0])
    nudging = jnp.stack([upper, jnp.zeros_like(upper)])
    target = (
        potential + time_step * tendency + nudging + noise_scale * perturb_now.astype(jnp.float32)
    )
    diagonal = 4.0 + layer_coupling()
    for sweep_no in range(SWEEPS):
        if sweep_no == 0:
            bordered = middle
        else:
            bordered = with_halo(stream, (("space", 1),), 1)
        stream = stream + (laplace_rim(bordered) + coupling(stream) - target) / diagonal
    return stream


def per_device(ensemble, offspring, new_owner, perturb, observed, nudge_rate):
    particles = offspring.shape[0]
    cumulative = jnp.cumsum(offspring)
    copy_index = jnp.arange(particles, dtype=jnp.int32)
    parent_copy = jnp.searchsorted(cumulative, copy_index, side="right")
    member_index = lax.axis_index("dom")
    parent = jnp.sum(jnp.where(new_owner == member_index, parent_copy, 0))
    shard_piece = lax.all_gather(ensemble, "dom", axis=0, tiled=True)
    labels = jnp.arange(shard_piece.shape[0], dtype=jnp.int32)
    picked = jnp.where((labels == parent)[:, None, None, None], shard_piece, 0.0)
    stream = jnp.sum(picked, axis=0)
    for step_no in range(STEPS):
        stream = model_step(stream, perturb[0, step_no], observed, nudge_rate)
    return stream[None]


def solution(mesh):
    in_specs = (
        P("dom", None, "space", None),
        P(),
        P(),
        P("dom", None, None, "space", None),
        P("space", None),
        P("space"),
    )
    out_specs = P("dom", None, "space", None)
    return jax.shard_map(
        per_device, mesh=mesh, in_specs=in_specs, out_specs=out_specs, check_vma=False
    )
```

profile of v0, /device:TPU:6, one launch (start us, length us, event | category | flops | bytes accessed | tf_op | source)
XLA Modules:
  0.0 166.2 jit_solution(12083379056018552837)
XLA Ops:
  8.3 5.8 %while.24 = (s32[]{:T(128)}, u32[64]{0:T(128)S(1)}, u32[64]{0:T(128)S(1)}, s32[64]{0:T(128)S(1)}, s32[]{:T(128)}, /*index=5*/s32[]{:T(128)}, s32[]{}) while((s32[]{:T(128)}, u32[64]{0:T(128)S(1)}, u32[64]{0:T(128)S(1)}, s32[64]{0:T(128)S(1)}, s32[]{:T(128)}, /*index=5*/s32[]{:T(128)}, s32[]{}) %tuple.53), condition=%wide.region_2.3_spmd.clone, body=%wide.region_1.2_spmd.clone.sunk | while | flops 1860 | bytes 7268 | solution.py:87
  8.3 0.8 gather_fusion
  9.1 0.8 gather_fusion
  10.0 0.8 gather_fusion
  10.8 0.8 gather_fusion
  11.6 0.8 gather_fusion
  12.5 0.8 gather_fusion
  13.3 0.8 gather_fusion
  14.1 1.3 fusion.83
  16.7 96.3 %all-gather.2.cloned.1.call-done = f32[64,2,8,4096]{3,2,1,0:T(8,128)} async-done(((f32[1,2,8,4096]{3,2,1,0:T(8,128)}), f32[64,2,8,4096]{3,2,1,0:T(8,128)}) %all-gather.2.cloned.1.call-update) | async-done | bytes 16777232 | tf_op jit(solution)/shard_map/all_gather | solution.py:90
  113.0 8.0 %select_reduce_fusion = f32[2,8,4096]{2,1,0:T(8,128)S(1)} fusion(f32[64,2,8,4096]{3,2,1,0:T(8,128)} %all-gather.2.cloned.1.call-done, pred[64]{0:T(512)(128)(4,1)S(1)} %iota_compare_fusion.1), kind=kLoop, calls=%fused_computation.9 | loop fusion | flops 8323072 | bytes 17039424 | tf_op jit(solution)/shard_map/reduce_sum | solution.py:93
  121.2 2.8 %collective-permute-start = (f32[2,2,4096]{2,1,0:T(2,128)S(1)}, f32[2,2,4096]{2,1,0:T(2,128)S(1)}, u32[]{:S(2)}, u32[]{:S(2)}) collective-permute-start(f32[2,2,4096]{2,1,0:T(2,128)S(1)} %get-tuple-element.133), channel_id=1, source_target_pairs={{1,0},{2,1},{3,2},{5,4},{6,5},{7,6},{9,8},{10,9},{11,10},{13,12},{... | collective-permute-start | bytes 196616 | tf_op jit(solution)/shard_map/ppermute | solution.py:23
  123.9 1.3 collective-permute-start.1
  125.8 4.3 %collective-permute-done.1 = f32[2,2,4096]{2,1,0:T(2,128)S(1)} collective-permute-done((f32[2,2,4096]{2,1,0:T(2,128)S(1)}, f32[2,2,4096]{2,1,0:T(2,128)S(1)}, u32[]{:S(2)}, u32[]{:S(2)}) %collective-permute-start.1) | collective-permute-done | bytes 65568 | tf_op jit(solution)/shard_map/ppermute | solution.py:20
  131.7 2.5 %collective-permute-start.2 = (f32[2,1,4096]{2,1,0:T(1,128)S(1)}, f32[2,1,4096]{2,1,0:T(1,128)S(1)}, u32[]{:S(2)}, u32[]{:S(2)}) collective-permute-start(f32[2,1,4096]{2,1,0:T(1,128)S(1)} %get-tuple-element.130), channel_id=1, source_target_pairs={{1,0},{2,1},{3,2},{5,4},{6,5},{7,6},{9,8},{10,9},{11,10},{13,12},{... | collective-permute-start | bytes 98312 | tf_op jit(solution)/shard_map/ppermute | solution.py:23
  134.2 1.3 collective-permute-start.3
  135.7 4.2 %collective-permute-done.3 = f32[2,1,4096]{2,1,0:T(1,128)S(1)} collective-permute-done((f32[2,1,4096]{2,1,0:T(1,128)S(1)}, f32[2,1,4096]{2,1,0:T(1,128)S(1)}, u32[]{:S(2)}, u32[]{:S(2)}) %collective-permute-start.3) | collective-permute-done | bytes 32800 | tf_op jit(solution)/shard_map/ppermute | solution.py:20
  140.5 2.5 %collective-permute-start.4 = (f32[2,2,4096]{2,1,0:T(2,128)S(1)}, f32[2,2,4096]{2,1,0:T(2,128)S(1)}, u32[]{:S(2)}, u32[]{:S(2)}) collective-permute-start(f32[2,2,4096]{2,1,0:T(2,128)S(1)} %get-tuple-element.121), channel_id=1, source_target_pairs={{1,0},{2,1},{3,2},{5,4},{6,5},{7,6},{9,8},{10,9},{11,10},{13,12},{... | collective-permute-start | bytes 196616 | tf_op jit(solution)/shard_map/ppermute | solution.py:23
  142.9 1.3 collective-permute-start.5
  144.8 4.3 %collective-permute-done.5 = f32[2,2,4096]{2,1,0:T(2,128)S(1)} collective-permute-done((f32[2,2,4096]{2,1,0:T(2,128)S(1)}, f32[2,2,4096]{2,1,0:T(2,128)S(1)}, u32[]{:S(2)}, u32[]{:S(2)}) %collective-permute-start.5) | collective-permute-done | bytes 65568 | tf_op jit(solution)/shard_map/ppermute | solution.py:20
  150.7 1.9 %collective-permute-start.6 = (f32[2,1,4096]{2,1,0:T(1,128)S(1)}, f32[2,1,4096]{2,1,0:T(1,128)S(1)}, u32[]{:S(2)}, u32[]{:S(2)}) collective-permute-start(f32[2,1,4096]{2,1,0:T(1,128)S(1)} %get-tuple-element.118), channel_id=1, source_target_pairs={{1,0},{2,1},{3,2},{5,4},{6,5},{7,6},{9,8},{10,9},{11,10},{13,12},{... | collective-permute-start | bytes 98312 | tf_op jit(solution)/shard_map/ppermute | solution.py:23
  152.6 1.3 collective-permute-start.7
  154.2 4.2 %collective-permute-done.7 = f32[2,1,4096]{2,1,0:T(1,128)S(1)} collective-permute-done((f32[2,1,4096]{2,1,0:T(1,128)S(1)}, f32[2,1,4096]{2,1,0:T(1,128)S(1)}, u32[]{:S(2)}, u32[]{:S(2)}) %collective-permute-start.7) | collective-permute-done | bytes 32800 | tf_op jit(solution)/shard_map/ppermute | solution.py:20
  158.4 0.9 fusion.42
  (74 shorter events, 8.6 us)
Async XLA Ops:
  6.5 123.9 %copy-start.2 = (f32[2]{0:T(128)S(1)}, f32[2]{0:T(128)}, u32[]{:S(2)}) copy-start(f32[2]{0:T(128)} %constant.71.clone) | copy-start | bytes 28
  6.5 124.5 %copy-start.4 = (f32[2]{0:T(128)S(1)}, f32[2]{0:T(128)}, u32[]{:S(2)}) copy-start(f32[2]{0:T(128)} %constant.72.clone) | copy-start | bytes 28
  6.5 124.5 %copy-start.3 = (f32[2]{0:T(128)S(1)}, f32[2]{0:T(128)}, u32[]{:S(2)}) copy-start(f32[2]{0:T(128)} %constant.80) | copy-start | bytes 28
  6.5 118.7 %copy-start = (f32[8,4096]{1,0:T(8,128)S(1)}, f32[8,4096]{1,0:T(8,128)}, u32[]{:S(2)}) copy-start(f32[8,4096]{1,0:T(8,128)} %param.22) | copy-start | bytes 393220
  6.5 124.5 %copy-start.1 = (bf16[1,2,2,8,4096]{4,3,2,1,0:T(8,128)(2,1)S(1)}, bf16[1,2,2,8,4096]{4,3,2,1,0:T(8,128)(2,1)}, u32[]{:S(2)}) copy-start(bf16[1,2,2,8,4096]{4,3,2,1,0:T(8,128)(2,1)} %param.21) | copy-start | bytes 786436
  6.5 106.5 %all-gather.2.cloned.1.call-start = ((), (), s32[]{:S(2)}) async-start(), calls=%async_computation | async-start | bytes 17039360 | tf_op jit(solution)/shard_map/all_gather | solution.py:90
  121.2 4.7 %collective-permute-start = (f32[2,2,4096]{2,1,0:T(2,128)S(1)}, f32[2,2,4096]{2,1,0:T(2,128)S(1)}, u32[]{:S(2)}, u32[]{:S(2)}) collective-permute-start(f32[2,2,4096]{2,1,0:T(2,128)S(1)} %get-tuple-element.133), channel_id=1, source_target_pairs={{1,0},{2,1},{3,2},{5,4},{6,5},{7,6},{9,8},{10,9},{11,10},{13,12},{... | collective-permute-start | bytes 196616 | tf_op jit(solution)/shard_map/ppermute | solution.py:23
  123.9 6.2 %collective-permute-start.1 = (f32[2,2,4096]{2,1,0:T(2,128)S(1)}, f32[2,2,4096]{2,1,0:T(2,128)S(1)}, u32[]{:S(2)}, u32[]{:S(2)}) collective-permute-start(f32[2,2,4096]{2,1,0:T(2,128)S(1)} %get-tuple-element.132), channel_id=1, source_target_pairs={{0,1},{1,2},{2,3},{4,5},{5,6},{6,7},{8,9},{9,10},{10,11},{12,13},{... | collective-permute-start | bytes 196616 | tf_op jit(solution)/shard_map/ppermute | solution.py:20
  131.7 4.1 %collective-permute-start.2 = (f32[2,1,4096]{2,1,0:T(1,128)S(1)}, f32[2,1,4096]{2,1,0:T(1,128)S(1)}, u32[]{:S(2)}, u32[]{:S(2)}) collective-permute-start(f32[2,1,4096]{2,1,0:T(1,128)S(1)} %get-tuple-element.130), channel_id=1, source_target_pairs={{1,0},{2,1},{3,2},{5,4},{6,5},{7,6},{9,8},{10,9},{11,10},{13,12},{... | collective-permute-start | bytes 98312 | tf_op jit(solution)/shard_map/ppermute | solution.py:23
  134.2 5.8 %collective-permute-start.3 = (f32[2,1,4096]{2,1,0:T(1,128)S(1)}, f32[2,1,4096]{2,1,0:T(1,128)S(1)}, u32[]{:S(2)}, u32[]{:S(2)}) collective-permute-start(f32[2,1,4096]{2,1,0:T(1,128)S(1)} %get-tuple-element.131), channel_id=1, source_target_pairs={{0,1},{1,2},{2,3},{4,5},{5,6},{6,7},{8,9},{9,10},{10,11},{12,13},{... | collective-permute-start | bytes 98312 | tf_op jit(solution)/shard_map/ppermute | solution.py:20
  140.5 4.4 %collective-permute-start.4 = (f32[2,2,4096]{2,1,0:T(2,128)S(1)}, f32[2,2,4096]{2,1,0:T(2,128)S(1)}, u32[]{:S(2)}, u32[]{:S(2)}) collective-permute-start(f32[2,2,4096]{2,1,0:T(2,128)S(1)} %get-tuple-element.121), channel_id=1, source_target_pairs={{1,0},{2,1},{3,2},{5,4},{6,5},{7,6},{9,8},{10,9},{11,10},{13,12},{... | collective-permute-start | bytes 196616 | tf_op jit(solution)/shard_map/ppermute | solution.py:23
  142.9 6.2 %collective-permute-start.5 = (f32[2,2,4096]{2,1,0:T(2,128)S(1)}, f32[2,2,4096]{2,1,0:T(2,128)S(1)}, u32[]{:S(2)}, u32[]{:S(2)}) collective-permute-start(f32[2,2,4096]{2,1,0:T(2,128)S(1)} %get-tuple-element.120), channel_id=1, source_target_pairs={{0,1},{1,2},{2,3},{4,5},{5,6},{6,7},{8,9},{9,10},{10,11},{12,13},{... | collective-permute-start | bytes 196616 | tf_op jit(solution)/shard_map/ppermute | solution.py:20
  150.7 3.5 %collective-permute-start.6 = (f32[2,1,4096]{2,1,0:T(1,128)S(1)}, f32[2,1,4096]{2,1,0:T(1,128)S(1)}, u32[]{:S(2)}, u32[]{:S(2)}) collective-permute-start(f32[2,1,4096]{2,1,0:T(1,128)S(1)} %get-tuple-element.118), channel_id=1, source_target_pairs={{1,0},{2,1},{3,2},{5,4},{6,5},{7,6},{9,8},{10,9},{11,10},{13,12},{... | collective-permute-start | bytes 98312 | tf_op jit(solution)/shard_map/ppermute | solution.py:23
  152.6 5.8 %collective-permute-start.7 = (f32[2,1,4096]{2,1,0:T(1,128)S(1)}, f32[2,1,4096]{2,1,0:T(1,128)S(1)}, u32[]{:S(2)}, u32[]{:S(2)}) collective-permute-start(f32[2,1,4096]{2,1,0:T(1,128)S(1)} %get-tuple-element.119), channel_id=1, source_target_pairs={{0,1},{1,2},{2,3},{4,5},{5,6},{6,7},{8,9},{9,10},{10,11},{12,13},{... | collective-permute-start | bytes 98312 | tf_op jit(solution)/shard_map/ppermute | solution.py:20
Sparse Core Ops, SparseCore 0:
  10.2 102.8 all-gather.1
where the time goes:
time: 167 us; the launch traced here: 166 us
  waiting for transfers between devices  115 us (69%)
  starting transfers between devices  14.8 us (9%)
  other arithmetic  14.1 us (8%)
  between operations  13.7 us (8%)
  local copies, waits for them, and re-layouts  8.09 us (5%)
    all_gather x1, waiting for transfers between devices, per_device(): shard_piece = lax.all_gather(ensemble, 'dom', axis=0, tiled=True)  96.3 us
    ppermute x4, waiting for transfers between devices, with_halo(): lax.ppermute(lax.slice_in_dim(block, block.shape[dim] - width, None, axis...  17 us
    ppermute x4, starting transfers between devices, with_halo(): lax.ppermute(lax.slice_in_dim(block, 0, width, axis=dim), axis, backward)  9.61 us
    reduce_sum x1, other arithmetic, per_device(): stream = jnp.sum(picked, axis=0)  7.98 us
    gather x7, local copies, waits for them, and re-layouts, per_device(): parent_copy = jnp.searchsorted(cumulative, copy_index, side='right')  5.44 us
    ppermute x4, starting transfers between devices, with_halo(): lax.ppermute(lax.slice_in_dim(block, block.shape[dim] - width, None, axis...  5.17 us
  transfers between devices with their start and end apart: 9, of which 9 were waited for; matrix products, arithmetic and copies ran while one was open for 6% of the time, Pallas kernels for 0%

commit v1 on v0

v1 whole, which is shorter than its diff:
```python
import functools

import jax
import jax.numpy as jnp
from jax import lax
from jax.experimental import pallas as pl
from jax.experimental.pallas import tpu as pltpu
from jax.sharding import PartitionSpec as P

STEPS = 2
COLS = 4096
ROWS = 8
MEMBERS = 64
LANES = 128
CHUNK = 512
COUPLE = (0.4, 0.6)
DRAG = (0.0, 0.2)
DT = 0.05
BETA = 1.0
NOISE = 0.5
F32 = jnp.float32


def sublane(shape):
    return lax.broadcasted_iota(jnp.int32, shape, len(shape) - 2)


def tile_of(device):
    return lax.rem(device, 2), pl.multiple_of(lax.div(device, 2) * LANES, LANES)


def partner(step, me):
    group, within = lax.div(step, 8), lax.rem(lax.rem(step, 8) + 1, 8)
    spread = lax.div(group + 1, 2)
    dz = jnp.where(lax.rem(group, 2) == 1, 4 - spread, 4 + spread)
    z, y, core = lax.div(me, 8), lax.rem(lax.div(me, 2), 4), lax.rem(me, 2)
    z = lax.rem(z + dz, 8)
    y = lax.rem(y + lax.div(within, 2), 4)
    core = lax.rem(core + lax.rem(within, 2), 2)
    return (z * 4 + y) * 2 + core


def window(ref, layer, start):
    left = pl.multiple_of(lax.rem(start + COLS - LANES, COLS), LANES)
    right = pl.multiple_of(lax.rem(start + CHUNK, COLS), LANES)
    return (
        ref[layer, :, pl.ds(left, LANES)],
        ref[layer, :, pl.ds(start, CHUNK)],
        ref[layer, :, pl.ds(right, LANES)],
    )


def west(parts):
    both = jnp.concatenate([parts[0], parts[1]], axis=1)
    return pltpu.roll(both, 1, 1)[:, LANES:]


def east(parts):
    both = jnp.concatenate([parts[1], parts[2]], axis=1)
    return pltpu.roll(both, CHUNK + LANES - 1, 1)[:, :CHUNK]


def up_of(value):
    return pltpu.roll(value, 1, 0)


def down_of(value):
    return pltpu.roll(value, ROWS - 1, 0)


def rows_beside(own, halo, outer):
    at = sublane(own.shape)
    up_o, up_h, down_o, down_h = up_of(own), up_of(halo), down_of(own), down_of(halo)
    above_o = jnp.where(at == 0, up_h, up_o)
    below_o = jnp.where(at == 7, down_h, down_o)
    above_h = jnp.where(at == 0, up_o, up_h)
    below_h = jnp.where(at == 7, down_o, down_h)
    if outer is None:
        return (above_o, above_h), (below_o, below_h)
    up_t, down_t = up_of(outer), down_of(outer)
    above_h = jnp.where(at == 4, up_t, above_h)
    below_h = jnp.where(at == 3, down_t, below_h)
    above_t = jnp.where(at == 4, up_h, up_t)
    below_t = jnp.where(at == 3, down_h, down_t)
    return (above_o, above_h, above_t), (below_o, below_h, below_t)


def laplace(parts, above, below):
    return above + below + west(parts) + east(parts) - 4.0 * parts[1]


def model_step(s, q, target, s1, force, pull, inside, step_no, last):
    n_q = 2 if last else 3
    chunks = COLS // CHUNK

    def vorticity(k, carry):
        start = pl.multiple_of(k * CHUNK, CHUNK)
        parts = [[window(s[i], layer, start) for i in range(n_q)] for layer in range(2)]
        for layer in range(2):
            mine = parts[layer]
            centre = [p[1] for p in mine] + [None] * (3 - n_q)
            above, below = rows_beside(*centre)
            for i in range(n_q):
                value = laplace(mine[i], above[i], below[i]) + COUPLE[layer] * (
                    parts[1 - layer][i][1] - mine[i][1]
                )
                if i:
                    value = jnp.where(inside, value, 0.0)
                q[i][layer, :, pl.ds(start, CHUNK)] = value
        return carry

    def first_sweep(k, carry):
        start = pl.multiple_of(k * CHUNK, CHUNK)
        here = pl.ds(start, CHUNK)
        for layer in range(2):
            s_parts = [window(s[i], layer, start) for i in range(2)]
            q_parts = [window(q[i], layer, start) for i in range(2)]
            s_outer = None if last else s[2][layer, :, here]
            q_outer = None if last else q[2][layer, :, here]
            s_above, s_below = rows_beside(s_parts[0][1], s_parts[1][1], s_outer)
            q_above, q_below = rows_beside(q_parts[0][1], q_parts[1][1], q_outer)
            for i in range(2):
                state, vort = s_parts[i][1], q_parts[i][1]
                ex_s = east(s_parts[i]) - west(s_parts[i])
                ex_q = east(q_parts[i]) - west(q_parts[i])
                ny_s = s_below[i] - s_above[i]
                ny_q = q_below[i] - q_above[i]
                tendency = (ny_s * ex_q - ex_s * ny_q) * 0.25 - (BETA * 0.5) * ex_s
                if DRAG[layer]:
                    tendency = tendency - DRAG[layer] * vort
                change = DT * tendency + force[i][step_no, layer, :, here]
                if layer == 0:
                    change = change - pull[i][:, 0:1] * state
                target[i][layer, :, here] = vort + change
                value = state - change * (1.0 / (4.0 + COUPLE[layer]))
                if i:
                    value = jnp.where(inside, value, 0.0)
                s1[i][layer, :, here] = value
        return carry

    def second_sweep(k, carry):
        start = pl.multiple_of(k * CHUNK, CHUNK)
        here = pl.ds(start, CHUNK)
        parts = [[window(s1[i], layer, start) for i in range(2)] for layer in range(2)]
        for layer in range(2):
            mine = parts[layer]
            above, below = rows_beside(mine[0][1], mine[1][1], None)
            for i in range(1 if last else 2):
                centre = mine[i][1]
                rest = (
                    laplace(mine[i], above[i], below[i])
                    + COUPLE[layer] * (parts[1 - layer][i][1] - centre)
                    - target[i][layer, :, here]
                )
                value = centre + rest * (1.0 / (4.0 + COUPLE[layer]))
                if i:
                    value = jnp.where(inside, value, 0.0)
                s[i][layer, :, here] = value
        return carry

    lax.fori_loop(0, chunks, vorticity, 0)
    lax.fori_loop(0, chunks, first_sweep, 0)
    lax.fori_loop(0, chunks, second_sweep, 0)


def kernel(
    offspring, new_owner, nudge, ensemble, perturb, observed, out,
    own_state, noise, obs, tiles, picked, parent_row, parent_at,
    s_own, s_halo, s_outer, q_own, q_halo, q_outer, s1_own, s1_halo,
    target_own, target_halo, force_own, force_halo, pull_own, pull_halo,
    local_sem, send_sem, recv_sem, row_send, row_recv,
):
    me, x = lax.axis_index("dom"), lax.axis_index("space")
    next_x, prev_x = lax.rem(x + 1, 4), lax.rem(x + 3, 4)

    loads = [
        pltpu.make_async_copy(ensemble.at[0], own_state, local_sem.at[0]),
        pltpu.make_async_copy(perturb.at[0], noise, local_sem.at[1]),
        pltpu.make_async_copy(observed, obs, local_sem.at[2]),
    ]
    for load in loads:
        load.start()

    barrier = pltpu.get_barrier_semaphore()

    def greet(step, carry):
        pl.semaphore_signal(barrier, inc=1, device_id=(partner(step, me), x))
        return carry

    lax.fori_loop(0, MEMBERS - 1, greet, 0)
    pl.semaphore_signal(barrier, inc=1, device_id=(me, next_x))
    pl.semaphore_signal(barrier, inc=1, device_id=(me, prev_x))

    lane = lax.broadcasted_iota(jnp.int32, (8, LANES), 1)

    def find_copy(j, copy):
        return jnp.where(lane == new_owner[j], j, copy)

    copy = lax.fori_loop(0, MEMBERS, find_copy, jnp.zeros((8, LANES), jnp.int32))

    def find_parent(i, carry):
        total, parent = carry
        total = total + offspring[i]
        return total, parent + (total <= copy).astype(jnp.int32)

    _, parent = lax.fori_loop(
        0, MEMBERS, find_parent, (jnp.int32(0), jnp.zeros((8, LANES), jnp.int32))
    )
    parent_row[...] = jnp.minimum(parent, MEMBERS - 1)
    to_scalars = pltpu.make_async_copy(parent_row, parent_at, local_sem.at[3])
    to_scalars.start()

    at = sublane((ROWS, LANES))
    rate = jnp.zeros((ROWS, LANES), F32)
    for r in range(ROWS):
        rate = jnp.where(at == r, DT * nudge[r], rate)
    pull_own[...] = rate
    loads[1].wait()
    loads[2].wait()

    def forcing(k, carry):
        here = pl.ds(pl.multiple_of(k * CHUNK, CHUNK), CHUNK)
        drawn = rate[:, 0:1] * obs[:, here]
        for t in range(STEPS):
            for layer in range(2):
                value = NOISE * noise[t, layer, :, here].astype(F32)
                force_own[t, layer, :, here] = value + drawn if layer == 0 else value
        return carry

    lax.fori_loop(0, COLS // CHUNK, forcing, 0)
    loads[0].wait()
    pl.semaphore_wait(barrier, MEMBERS + 1)

    def spread(step, carry):
        to = partner(step, me)
        layer, start = tile_of(to)
        pltpu.make_async_remote_copy(
            src_ref=own_state.at[layer, :, pl.ds(start, LANES)],
            dst_ref=tiles.at[me],
            send_sem=send_sem.at[0],
            recv_sem=recv_sem.at[0],
            device_id=(to, x),
        ).start()
        return carry

    lax.fori_loop(0, MEMBERS - 1, spread, 0)

    def row_copy(src, dst, number, to_x):
        return pltpu.make_async_remote_copy(
            src_ref=src,
            dst_ref=dst,
            send_sem=row_send.at[number],
            recv_sem=row_recv.at[number],
            device_id=(me, to_x),
        )

    low, high = pl.ds(0, 4), pl.ds(4, 4)
    early = [
        row_copy(force_own.at[0, :, low], force_halo.at[0, :, low], 0, prev_x),
        row_copy(force_own.at[0, :, high], force_halo.at[0, :, high], 1, next_x),
        row_copy(force_own.at[1, :, pl.ds(0, 1)], force_halo.at[1, :, pl.ds(0, 1)], 2, prev_x),
        row_copy(force_own.at[1, :, pl.ds(7, 1)], force_halo.at[1, :, pl.ds(7, 1)], 3, next_x),
        row_copy(pull_own.at[low], pull_halo.at[low], 4, prev_x),
        row_copy(pull_own.at[high], pull_halo.at[high], 5, next_x),
    ]
    for one in early:
        one.start()

    my_layer, my_start = tile_of(me)
    tiles[me] = own_state[my_layer, :, pl.ds(my_start, LANES)]
    to_scalars.wait()

    def all_tiles(sem):
        return pltpu.make_async_copy(
            tiles.at[pl.ds(0, MEMBERS - 1)], tiles.at[pl.ds(0, MEMBERS - 1)], sem
        )

    all_tiles(recv_sem.at[0]).wait()

    def choose(m, carry):
        picked[m] = tiles[parent_at[0, m]]
        return carry

    lax.fori_loop(0, MEMBERS, choose, 0)

    def deliver(step, carry):
        to = partner(step, me)
        pltpu.make_async_remote_copy(
            src_ref=picked.at[to],
            dst_ref=s_own.at[my_layer, :, pl.ds(my_start, LANES)],
            send_sem=send_sem.at[1],
            recv_sem=recv_sem.at[1],
            device_id=(to, x),
        ).start()
        return carry

    lax.fori_loop(0, MEMBERS - 1, deliver, 0)
    s_own[my_layer, :, pl.ds(my_start, LANES)] = picked[me]
    all_tiles(recv_sem.at[1]).wait()

    states = [
        row_copy(s_own.at[:, low], s_halo.at[:, low], 6, prev_x),
        row_copy(s_own.at[:, high], s_halo.at[:, high], 7, next_x),
        row_copy(s_own.at[:, pl.ds(4, 2)], s_outer.at[:, pl.ds(4, 2)], 8, prev_x),
        row_copy(s_own.at[:, pl.ds(2, 2)], s_outer.at[:, pl.ds(2, 2)], 9, next_x),
    ]
    for one in states:
        one.start()
    all_tiles(send_sem.at[0]).wait()
    all_tiles(send_sem.at[1]).wait()
    for one in early + states:
        one.wait()

    wide = sublane((ROWS, CHUNK))
    inside = jnp.where(wide < 4, jnp.where(x < 3, 1, 0), jnp.where(x > 0, 1, 0)) == 1

    def clear(k, carry):
        here = pl.ds(pl.multiple_of(k * CHUNK, CHUNK), CHUNK)
        for layer in range(2):
            for ref in (s_halo, s_outer):
                ref[layer, :, here] = jnp.where(inside, ref[layer, :, here], 0.0)
        return carry

    lax.fori_loop(0, COLS // CHUNK, clear, 0)

    s, q = (s_own, s_halo, s_outer), (q_own, q_halo, q_outer)
    target, s1 = (target_own, target_halo), (s1_own, s1_halo)
    force, pull = (force_own, force_halo), (pull_own, pull_halo)
    for t in range(STEPS):
        model_step(s, q, target, s1, force, pull, inside, t, t == STEPS - 1)

    result = pltpu.make_async_copy(s_own, out.at[0], local_sem.at[0])
    result.start()
    result.wait()


def per_device(ensemble, offspring, new_owner, perturb, observed, nudge_rate):
    layers = pltpu.VMEM((2, ROWS, COLS), F32)
    forces = pltpu.VMEM((STEPS, 2, ROWS, COLS), F32)
    small = pltpu.VMEM((ROWS, LANES), F32)
    tiles = pltpu.VMEM((MEMBERS, 8, LANES), F32)
    return pl.pallas_call(
        kernel,
        out_shape=jax.ShapeDtypeStruct(ensemble.shape, F32),
        in_specs=[pl.BlockSpec(memory_space=pltpu.SMEM)] * 3
        + [pl.BlockSpec(memory_space=pl.ANY)] * 3,
        out_specs=pl.BlockSpec(memory_space=pl.ANY),
        scratch_shapes=[
            layers,
            pltpu.VMEM((STEPS, 2, ROWS, COLS), jnp.bfloat16),
            pltpu.VMEM((ROWS, COLS), F32),
            tiles,
            tiles,
            pltpu.VMEM((8, LANES), jnp.int32),
            pltpu.SMEM((8, LANES), jnp.int32),
            *[layers] * 10,
            forces,
            forces,
            small,
            small,
            pltpu.SemaphoreType.DMA((4,)),
            pltpu.SemaphoreType.DMA((2,)),
            pltpu.SemaphoreType.DMA((2,)),
            pltpu.SemaphoreType.DMA((10,)),
            pltpu.SemaphoreType.DMA((10,)),
        ],
        compiler_params=pltpu.CompilerParams(
            collective_id=0, has_side_effects=True, vmem_limit_bytes=32 * 1024 * 1024
        ),
        name="filter_step",
    )(offspring, new_owner, nudge_rate, ensemble, perturb, observed)


def solution(mesh):
    in_specs = (
        P("dom", None, "space", None),
        P(),
        P(),
        P("dom", None, None, "space", None),
        P("space", None),
        P("space"),
    )
    out_specs = P("dom", None, "space", None)
    return jax.shard_map(
        per_device, mesh=mesh, in_specs=in_specs, out_specs=out_specs, check_vma=False
    )
```

time: 167 us -> 50.6 us (0.30)
  the two profiles are of different devices: /device:TPU:6 before, /device:TPU:1 now
where the time goes in v1:
time: 50.6 us; the launch traced here: 50.4 us
  Pallas kernels  44.9 us (89%)
  local copies, waits for them, and re-layouts  5.47 us (11%)
    pallas_call x1, Pallas kernels, per_device(): pl.pallas_call(kernel, out_shape=jax.ShapeDtypeStruct(ensemble.shape, F32...  44.9 us
    unnamed x13, local copies, waits for them, and re-layouts  5.47 us

profile of v1, /device:TPU:1, one launch (start us, length us, event | category | flops | bytes accessed | tf_op | source)
XLA Modules:
  0.0 50.4 jit_solution(14431391530938288397)
XLA Ops:
  0.0 0.0 copy-start
  0.0 0.9 %copy-done = f32[1,2,8,4096]{3,2,1,0:T(8,128)S(1)} copy-done((f32[1,2,8,4096]{3,2,1,0:T(8,128)S(1)}, f32[1,2,8,4096]{3,2,1,0:T(8,128)}, u32[]{:S(2)}) %copy-start) | copy-done | bytes 262168
  1.0 0.0 copy-start.1
  1.0 0.9 %copy-done.1 = bf16[1,2,2,8,4096]{4,3,2,1,0:T(8,128)(2,1)S(1)} copy-done((bf16[1,2,2,8,4096]{4,3,2,1,0:T(8,128)(2,1)S(1)}, bf16[1,2,2,8,4096]{4,3,2,1,0:T(8,128)(2,1)}, u32[]{:S(2)}) %copy-start.1) | copy-done | bytes 262168
  1.9 0.0 copy-start.2
  1.9 0.9 %copy-done.2 = f32[8,4096]{1,0:T(8,128)S(1)} copy-done((f32[8,4096]{1,0:T(8,128)S(1)}, f32[8,4096]{1,0:T(8,128)}, u32[]{:S(2)}) %copy-start.2) | copy-done | bytes 131096
  2.8 0.0 copy-start.3
  2.8 0.7 %copy-done.3 = s32[64]{0:T(128)S(1)} copy-done((s32[64]{0:T(128)S(1)}, s32[64]{0:T(128)}, u32[]{:S(2)}) %copy-start.3) | copy-done | bytes 280
  3.5 0.0 copy-start.4
  3.5 0.7 %copy-done.4 = s32[64]{0:T(128)S(1)} copy-done((s32[64]{0:T(128)S(1)}, s32[64]{0:T(128)}, u32[]{:S(2)}) %copy-start.4) | copy-done | bytes 280
  4.1 0.0 copy-start.5
  4.1 0.7 %copy-done.5 = f32[8]{0:T(128)S(1)} copy-done((f32[8]{0:T(128)S(1)}, f32[8]{0:T(128)}, u32[]{:S(2)}) %copy-start.5) | copy-done | bytes 56
  4.8 44.9 %filter_step.1 = f32[1,2,8,4096]{3,2,1,0:T(8,128)S(1)} custom-call(s32[64]{0:T(128)S(1)} %copy-done.3, s32[64]{0:T(128)S(1)} %copy-done.4, f32[8]{0:T(128)S(1)} %copy-done.5, f32[1,2,8,4096]{3,2,1,0:T(8,128)S(1)} %copy-done, bf16[1,2,2,8,4096]{4,3,2,1,0:T(8,128)(2,1)S(1)} %copy-done.1, f32[8,4096]{1,0:T(8,128)S(1)} %copy-done.2), custom_call_target="tpu_custom_call" | custom-call | tf_op jit(solution)/shard_map/filter_step/pallas_call | solution.py:342
  49.7 0.7 %copy.8 = f32[1,2,8,4096]{3,2,1,0:T(8,128)} copy(f32[1,2,8,4096]{3,2,1,0:T(8,128)S(1)} %filter_step.1) | data formatting | bytes 524288
Async XLA Ops:
  0.0 0.9 %copy-start = (f32[1,2,8,4096]{3,2,1,0:T(8,128)S(1)}, f32[1,2,8,4096]{3,2,1,0:T(8,128)}, u32[]{:S(2)}) copy-start(f32[1,2,8,4096]{3,2,1,0:T(8,128)} %ensemble.1) | copy-start | bytes 786436
  1.0 0.9 %copy-start.1 = (bf16[1,2,2,8,4096]{4,3,2,1,0:T(8,128)(2,1)S(1)}, bf16[1,2,2,8,4096]{4,3,2,1,0:T(8,128)(2,1)}, u32[]{:S(2)}) copy-start(bf16[1,2,2,8,4096]{4,3,2,1,0:T(8,128)(2,1)} %perturb.1) | copy-start | bytes 786436
  1.9 0.9 %copy-start.2 = (f32[8,4096]{1,0:T(8,128)S(1)}, f32[8,4096]{1,0:T(8,128)}, u32[]{:S(2)}) copy-start(f32[8,4096]{1,0:T(8,128)} %observed.1) | copy-start | bytes 393220
  2.8 0.7 %copy-start.3 = (s32[64]{0:T(128)S(1)}, s32[64]{0:T(128)}, u32[]{:S(2)}) copy-start(s32[64]{0:T(128)} %offspring.1) | copy-start | bytes 772
  3.5 0.7 %copy-start.4 = (s32[64]{0:T(128)S(1)}, s32[64]{0:T(128)}, u32[]{:S(2)}) copy-start(s32[64]{0:T(128)} %new_owner.1) | copy-start | bytes 772
  4.1 0.7 %copy-start.5 = (f32[8]{0:T(128)S(1)}, f32[8]{0:T(128)}, u32[]{:S(2)}) copy-start(f32[8]{0:T(128)} %nudge.1) | copy-start | bytes 100

commit v2 on v0

v2 whole, which is shorter than its diff:
```python
import functools

import jax
import jax.numpy as jnp
from jax import lax
from jax.experimental import pallas as pl
from jax.experimental.pallas import tpu as pltpu
from jax.sharding import PartitionSpec as P

STEPS = 2
COLS = 4096
ROWS = 8
MEMBERS = 64
LANES = 128
PLANES = 8
PER_PLANE = 8
BAND = COLS // PLANES
PARTS = ((0, 4), (4, 4))
COUPLE = (0.4, 0.6)
DRAG = (0.0, 0.2)
DT = 0.05
BETA = 1.0
NOISE = 0.5
F32 = jnp.float32


def sublane(shape):
    return lax.broadcasted_iota(jnp.int32, shape, len(shape) - 2)


def west(value):
    return pltpu.roll(value, 1, 1)


def east(value):
    return pltpu.roll(value, COLS - 1, 1)


def up_of(value):
    return pltpu.roll(value, 1, 0)


def down_of(value):
    return pltpu.roll(value, ROWS - 1, 0)


def rows_beside(own, halo, outer):
    at = sublane(own.shape)
    up_o, up_h, down_o, down_h = up_of(own), up_of(halo), down_of(own), down_of(halo)
    above_o = jnp.where(at == 0, up_h, up_o)
    below_o = jnp.where(at == 7, down_h, down_o)
    above_h = jnp.where(at == 0, up_o, up_h)
    below_h = jnp.where(at == 7, down_o, down_h)
    if outer is None:
        return (above_o, above_h), (below_o, below_h)
    up_t, down_t = up_of(outer), down_of(outer)
    above_h = jnp.where(at == 4, up_t, above_h)
    below_h = jnp.where(at == 3, down_t, below_h)
    above_t = jnp.where(at == 4, up_h, up_t)
    below_t = jnp.where(at == 3, down_h, down_t)
    return (above_o, above_h, above_t), (below_o, below_h, below_t)


def laplace(value, above, below):
    return above + below + west(value) + east(value) - 4.0 * value


def model_step(s, q, target, s1, force, pull, inside, step_no, last):
    n_q = 2 if last else 3

    mine = [[s[i][layer] for i in range(n_q)] for layer in range(2)]
    for layer in range(2):
        above, below = rows_beside(*mine[layer], *[None] * (3 - n_q))
        for i in range(n_q):
            here, other = mine[layer][i], mine[1 - layer][i]
            value = laplace(here, above[i], below[i]) + COUPLE[layer] * (other - here)
            q[i][layer] = jnp.where(inside, value, 0.0) if i else value

    for layer in range(2):
        state, vort = [s[i][layer] for i in range(2)], [q[i][layer] for i in range(2)]
        s_above, s_below = rows_beside(*state, None if last else s[2][layer])
        q_above, q_below = rows_beside(*vort, None if last else q[2][layer])
        for i in range(2):
            ex_s = east(state[i]) - west(state[i])
            ex_q = east(vort[i]) - west(vort[i])
            ny_s = s_below[i] - s_above[i]
            ny_q = q_below[i] - q_above[i]
            tendency = (ny_s * ex_q - ex_s * ny_q) * 0.25 - (BETA * 0.5) * ex_s
            if DRAG[layer]:
                tendency = tendency - DRAG[layer] * vort[i]
            change = DT * tendency + force[i][step_no, layer]
            if layer == 0:
                change = change - pull[i][:, 0:1] * state[i]
            target[i][layer] = vort[i] + change
            value = state[i] - change * (1.0 / (4.0 + COUPLE[layer]))
            s1[i][layer] = jnp.where(inside, value, 0.0) if i else value

    mine = [[s1[i][layer] for i in range(2)] for layer in range(2)]
    for layer in range(2):
        above, below = rows_beside(*mine[layer], None)
        for i in range(1 if last else 2):
            here, other = mine[layer][i], mine[1 - layer][i]
            rest = (
                laplace(here, above[i], below[i])
                + COUPLE[layer] * (other - here)
                - target[i][layer]
            )
            value = here + rest * (1.0 / (4.0 + COUPLE[layer]))
            s[i][layer] = jnp.where(inside, value, 0.0) if i else value


def kernel(
    offspring_in, new_owner_in, nudge_in, ensemble, perturb, observed, out,
    offspring, new_owner, nudge, noise, obs, tiles_a, tiles_b, picked_a, picked_b,
    parent_row, parent_at,
    s_own, s_halo, s_outer, q_own, q_halo, q_outer, s1_own, s1_halo,
    target_own, target_halo, force_own, force_halo, pull_own, pull_halo,
    local_sem, spread_send, spread_recv, deliver_send, deliver_recv,
    early_send, early_recv, row_send, row_recv,
):
    me, x = lax.axis_index("dom"), lax.axis_index("space")
    next_x, prev_x = lax.rem(x + 1, 4), lax.rem(x + 3, 4)
    plane, y, core = lax.div(me, 8), lax.rem(lax.div(me, 2), 4), lax.rem(me, 2)
    tiles, picked = (tiles_a, tiles_b), (picked_a, picked_b)
    places = [
        (lax.rem(y + dy, 4) * 2 + lax.rem(core + dc, 2), lax.rem(y + dy, 4), lax.rem(core + dc, 2))
        for dy, dc in ((2, 1), (2, 0), (1, 1), (1, 0), (3, 1), (3, 0), (0, 1), (0, 0))
    ]

    def nth_plane(n):
        half = lax.div(n + 1, 2)
        return lax.rem(plane + jnp.where(lax.rem(n, 2) == 1, 4 - half, 4 + half), PLANES)

    def for_partners(act):
        def one_plane(n, carry, count=PER_PLANE):
            z = nth_plane(n)
            for place, at_y, at_core in places[:count]:
                act(z * PER_PLANE + place, at_core, pl.multiple_of((z * 4 + at_y) * LANES, LANES))
            return carry

        lax.fori_loop(0, PLANES - 1, one_plane, 0)
        one_plane(PLANES - 1, 0, PER_PLANE - 1)

    loads = [
        pltpu.make_async_copy(new_owner_in, new_owner, local_sem.at[0]),
        pltpu.make_async_copy(offspring_in, offspring, local_sem.at[1]),
        pltpu.make_async_copy(nudge_in, nudge, local_sem.at[2]),
        pltpu.make_async_copy(perturb.at[0], noise, local_sem.at[3]),
        pltpu.make_async_copy(observed, obs, local_sem.at[4]),
    ]
    for load in loads:
        load.start()

    barrier = pltpu.get_barrier_semaphore()
    for_partners(
        lambda to, layer, start: pl.semaphore_signal(barrier, inc=1, device_id=(to, x))
    )
    pl.semaphore_signal(barrier, inc=1, device_id=(me, next_x))
    pl.semaphore_signal(barrier, inc=1, device_id=(me, prev_x))
    pl.semaphore_wait(barrier, MEMBERS + 1)

    my_start = pl.multiple_of(lax.div(me, 2) * LANES, LANES)
    own_tiles = []
    for part, (row, count) in enumerate(PARTS):
        rows = pl.ds(row, count)

        def spread(to, layer, start, part=part, rows=rows):
            pltpu.make_async_remote_copy(
                src_ref=ensemble.at[0, layer, rows, pl.ds(start, LANES)],
                dst_ref=tiles[part].at[me, rows],
                send_sem=spread_send.at[part],
                recv_sem=spread_recv.at[part],
                device_id=(to, x),
            ).start()

        for_partners(spread)
        own = pltpu.make_async_copy(
            ensemble.at[0, core, rows, pl.ds(my_start, LANES)],
            tiles[part].at[me, rows],
            local_sem.at[5 + part],
        )
        own.start()
        own_tiles.append(own)

    for load in loads:
        load.wait()
    lane = lax.broadcasted_iota(jnp.int32, (8, LANES), 1)
    copy = jnp.zeros((8, LANES), jnp.int32)
    for j in range(MEMBERS):
        copy = jnp.where(lane == new_owner[j], j, copy)
    parent, total = jnp.zeros((8, LANES), jnp.int32), jnp.int32(0)
    for i in range(MEMBERS):
        total = total + offspring[i]
        parent = parent + (total <= copy).astype(jnp.int32)
    parent_row[...] = jnp.minimum(parent, MEMBERS - 1)
    to_scalars = pltpu.make_async_copy(parent_row, parent_at, local_sem.at[0])
    to_scalars.start()

    at = sublane((ROWS, LANES))
    rate = jnp.zeros((ROWS, LANES), F32)
    for r in range(ROWS):
        rate = jnp.where(at == r, DT * nudge[r], rate)
    pull_own[...] = rate
    drawn = rate[:, 0:1] * obs[...]
    for t in range(STEPS):
        for layer in range(2):
            value = NOISE * noise[t, layer].astype(F32)
            force_own[t, layer] = value + drawn if layer == 0 else value

    def early_copy(src, dst, number, to_x):
        return pltpu.make_async_remote_copy(
            src_ref=src,
            dst_ref=dst,
            send_sem=early_send.at[number],
            recv_sem=early_recv.at[number],
            device_id=(me, to_x),
        )

    low, high = pl.ds(0, 4), pl.ds(4, 4)
    early = [
        early_copy(force_own.at[0, :, low], force_halo.at[0, :, low], 0, prev_x),
        early_copy(force_own.at[0, :, high], force_halo.at[0, :, high], 1, next_x),
        early_copy(force_own.at[1, :, pl.ds(0, 1)], force_halo.at[1, :, pl.ds(0, 1)], 2, prev_x),
        early_copy(force_own.at[1, :, pl.ds(7, 1)], force_halo.at[1, :, pl.ds(7, 1)], 3, next_x),
        early_copy(pull_own.at[low], pull_halo.at[low], 4, prev_x),
        early_copy(pull_own.at[high], pull_halo.at[high], 5, next_x),
    ]
    for one in early:
        one.start()
    to_scalars.wait()

    def tiles_of(part, count):
        some = tiles[part].at[pl.ds(0, count), pl.ds(*PARTS[part])]
        return lambda sem: pltpu.make_async_copy(some, some, sem).wait()

    for part, (row, count) in enumerate(PARTS):
        rows = pl.ds(row, count)
        own_tiles[part].wait()
        tiles_of(part, MEMBERS - 1)(spread_recv.at[part])
        for m in range(MEMBERS):
            picked[part][m, rows] = tiles[part][parent_at[0, m], rows]

        def deliver(to, layer, start, part=part, rows=rows):
            pltpu.make_async_remote_copy(
                src_ref=picked[part].at[to, rows],
                dst_ref=s_own.at[core, rows, pl.ds(my_start, LANES)],
                send_sem=deliver_send.at[part],
                recv_sem=deliver_recv.at[part, plane],
                device_id=(to, x),
            ).start()

        for_partners(deliver)
        s_own[core, rows, pl.ds(my_start, LANES)] = picked[part][me, rows]

    def forward(part, z):
        band = pl.ds(pl.multiple_of(z * BAND, BAND), BAND)
        sides = (
            ((low, s_halo, prev_x, 0), (pl.ds(2, 2), s_outer, next_x, 1)),
            ((high, s_halo, next_x, 2), (pl.ds(4, 2), s_outer, prev_x, 3)),
        )[part]
        for rows, halo, to_x, number in sides:
            pltpu.make_async_remote_copy(
                src_ref=s_own.at[:, rows, band],
                dst_ref=halo.at[:, rows, band],
                send_sem=row_send.at[number],
                recv_sem=row_recv.at[number],
                device_id=(me, to_x),
            ).start()

    for part in range(len(PARTS)):

        def pass_on(n, carry, part=part, count=PER_PLANE):
            z = nth_plane(n)
            tiles_of(part, count)(deliver_recv.at[part, z])
            forward(part, z)
            return carry

        lax.fori_loop(0, PLANES - 1, pass_on, 0)
        pass_on(PLANES - 1, 0, count=PER_PLANE - 1)

    for part in range(len(PARTS)):
        tiles_of(part, MEMBERS - 1)(spread_send.at[part])
        tiles_of(part, MEMBERS - 1)(deliver_send.at[part])
    for one in early:
        one.wait()
    for number, count in enumerate((4, 2, 4, 2)):
        some = s_own.at[:, pl.ds(0, count)]
        for sem in (row_recv, row_send):
            pltpu.make_async_copy(some, some, sem.at[number]).wait()

    wide = sublane((ROWS, COLS))
    inside = jnp.where(wide < 4, jnp.where(x < 3, 1, 0), jnp.where(x > 0, 1, 0)) == 1
    for ref in (s_halo, s_outer):
        for layer in range(2):
            ref[layer] = jnp.where(inside, ref[layer], 0.0)

    s, q = (s_own, s_halo, s_outer), (q_own, q_halo, q_outer)
    target, s1 = (target_own, target_halo), (s1_own, s1_halo)
    force, pull = (force_own, force_halo), (pull_own, pull_halo)
    for t in range(STEPS):
        model_step(s, q, target, s1, force, pull, inside, t, t == STEPS - 1)

    result = pltpu.make_async_copy(s_own, out.at[0], local_sem.at[0])
    result.start()
    result.wait()


def per_device(ensemble, offspring, new_owner, perturb, observed, nudge_rate):
    layers = pltpu.VMEM((2, ROWS, COLS), F32)
    forces = pltpu.VMEM((STEPS, 2, ROWS, COLS), F32)
    small = pltpu.VMEM((ROWS, LANES), F32)
    tiles = pltpu.VMEM((MEMBERS, 8, LANES), F32)
    dma = pltpu.SemaphoreType.DMA
    return pl.pallas_call(
        kernel,
        out_shape=jax.ShapeDtypeStruct(ensemble.shape, F32),
        in_specs=[pl.BlockSpec(memory_space=pltpu.HBM)] * 6,
        out_specs=pl.BlockSpec(memory_space=pltpu.HBM),
        scratch_shapes=[
            pltpu.SMEM((MEMBERS,), jnp.int32),
            pltpu.SMEM((MEMBERS,), jnp.int32),
            pltpu.SMEM((ROWS,), F32),
            pltpu.VMEM((STEPS, 2, ROWS, COLS), jnp.bfloat16),
            pltpu.VMEM((ROWS, COLS), F32),
            *[tiles] * 4,
            pltpu.VMEM((8, LANES), jnp.int32),
            pltpu.SMEM((8, LANES), jnp.int32),
            *[layers] * 10,
            forces,
            forces,
            small,
            small,
            dma((7,)),
            dma((2,)),
            dma((2,)),
            dma((2,)),
            dma((2, PLANES)),
            dma((6,)),
            dma((6,)),
            dma((4,)),
            dma((4,)),
        ],
        compiler_params=pltpu.CompilerParams(
            collective_id=0, has_side_effects=True, vmem_limit_bytes=60 * 1024 * 1024
        ),
        name="filter_step",
    )(offspring, new_owner, nudge_rate, ensemble, perturb, observed)


def solution(mesh):
    in_specs = (
        P("dom", None, "space", None),
        P(),
        P(),
        P("dom", None, None, "space", None),
        P("space", None),
        P("space"),
    )
    out_specs = P("dom", None, "space", None)
    return jax.shard_map(
        per_device, mesh=mesh, in_specs=in_specs, out_specs=out_specs, check_vma=False
    )
```

time: 167 us -> 39.1 us (0.23)
  the two profiles are of different devices: /device:TPU:6 before, /device:TPU:1 now
where the time goes in v2:
time: 39.1 us; the launch traced here: 39 us
  Pallas kernels  37.3 us (95%)
  local copies, waits for them, and re-layouts  1.67 us (4%)
    pallas_call x1, Pallas kernels, per_device(): pl.pallas_call(kernel, out_shape=jax.ShapeDtypeStruct(ensemble.shape, F32...  37.3 us
    unnamed x1, local copies, waits for them, and re-layouts  1.67 us

profile of v2, /device:TPU:1, one launch (start us, length us, event | category | flops | bytes accessed | tf_op | source)
XLA Modules:
  0.0 39.0 jit_solution(13188757668775997854)
XLA Ops:
  0.0 37.3 %filter_step.1 = f32[1,2,8,4096]{3,2,1,0:T(8,128)} custom-call(s32[64]{0:T(128)} %offspring_in.1, s32[64]{0:T(128)} %new_owner_in.1, f32[8]{0:T(128)} %nudge_in.1, f32[1,2,8,4096]{3,2,1,0:T(8,128)} %ensemble.1, bf16[1,2,2,8,4096]{4,3,2,1,0:T(8,128)(2,1)} %perturb.1, f32[8,4096]{1,0:T(8,128)} %observed.1), custom_call_target="tpu_custom_call" | custom-call | tf_op jit(solution)/shard_map/filter_step/pallas_call | solution.py:314
  37.3 1.7 %copy.8 = f32[1,2,8,4096]{3,2,1,0:T(8,128)} copy(f32[1,2,8,4096]{3,2,1,0:T(8,128)} %filter_step.1) | data formatting | bytes 524288

commit v3 on v2

--- a/solution.py
+++ b/solution.py
@@ -65,7 +65,7 @@
     return above + below + west(value) + east(value) - 4.0 * value
 
 
-def model_step(s, q, target, s1, force, pull, inside, step_no, last):
+def model_step(s, q, target, s1, force, pull, inside, step_no, last, out):
     n_q = 2 if last else 3
 
     mine = [[s[i][layer] for i in range(n_q)] for layer in range(2)]
@@ -106,7 +106,10 @@
                 - target[i][layer]
             )
             value = here + rest * (1.0 / (4.0 + COUPLE[layer]))
-            s[i][layer] = jnp.where(inside, value, 0.0) if i else value
+            if last:
+                out[0, layer] = value
+            else:
+                s[i][layer] = jnp.where(inside, value, 0.0) if i else value
 
 
 def kernel(
@@ -298,11 +301,7 @@
     target, s1 = (target_own, target_halo), (s1_own, s1_halo)
     force, pull = (force_own, force_halo), (pull_own, pull_halo)
     for t in range(STEPS):
-        model_step(s, q, target, s1, force, pull, inside, t, t == STEPS - 1)
-
-    result = pltpu.make_async_copy(s_own, out.at[0], local_sem.at[0])
-    result.start()
-    result.wait()
+        model_step(s, q, target, s1, force, pull, inside, t, t == STEPS - 1, out)
 
 
 def per_device(ensemble, offspring, new_owner, perturb, observed, nudge_rate):
@@ -311,11 +310,15 @@
     small = pltpu.VMEM((ROWS, LANES), F32)
     tiles = pltpu.VMEM((MEMBERS, 8, LANES), F32)
     dma = pltpu.SemaphoreType.DMA
+    operands = [
+        pltpu.with_memory_space_constraint(a, pltpu.HBM)
+        for a in (offspring, new_owner, nudge_rate, ensemble, perturb, observed)
+    ]
     return pl.pallas_call(
         kernel,
-        out_shape=jax.ShapeDtypeStruct(ensemble.shape, F32),
+        out_shape=pltpu.VMEM(ensemble.shape, F32),
         in_specs=[pl.BlockSpec(memory_space=pltpu.HBM)] * 6,
-        out_specs=pl.BlockSpec(memory_space=pltpu.HBM),
+        out_specs=pl.BlockSpec(memory_space=pltpu.VMEM),
         scratch_shapes=[
             pltpu.SMEM((MEMBERS,), jnp.int32),
             pltpu.SMEM((MEMBERS,), jnp.int32),
@@ -341,10 +344,10 @@
             dma((4,)),
         ],
         compiler_params=pltpu.CompilerParams(
-            collective_id=0, has_side_effects=True, vmem_limit_bytes=60 * 1024 * 1024
+            collective_id=0, has_side_effects=True, vmem_limit_bytes=48 * 1024 * 1024
         ),
         name="filter_step",
-    )(offspring, new_owner, nudge_rate, ensemble, perturb, observed)
+    )(*operands)
 
 
 def solution(mesh):

time: 39.1 us -> 37.4 us (0.957)
  local copies, waits for them, and re-layouts: 1.67 us -> 0.71 us
  Pallas kernels: 37.3 us -> 36.6 us
    unnamed x1, local copies, waits for them, and re-layouts: 1.67 us -> 0.71 us
    pallas_call x1, Pallas kernels: 37.3 us -> 36.6 us  [per_device(): pl.pallas_call(kernel, out_shape=pltpu.VMEM(ensemble.shape, F32), in_spec...]
where the time goes in v3:
time: 37.4 us; the launch traced here: 37.3 us
  Pallas kernels  36.6 us (98%)
  local copies, waits for them, and re-layouts  0.71 us (2%)
    pallas_call x1, Pallas kernels, per_device(): pl.pallas_call(kernel, out_shape=pltpu.VMEM(ensemble.shape, F32), in_spec...  36.6 us

profile of v3, /device:TPU:1, one launch (start us, length us, event | category | flops | bytes accessed | tf_op | source)
XLA Modules:
  0.0 37.3 jit_solution(2784712622866339275)
XLA Ops:
  0.0 36.6 %filter_step.1 = f32[1,2,8,4096]{3,2,1,0:T(8,128)S(1)} custom-call(s32[64]{0:T(128)} %offspring_in.1, s32[64]{0:T(128)} %new_owner_in.1, f32[8]{0:T(128)} %nudge_in.1, f32[1,2,8,4096]{3,2,1,0:T(8,128)} %ensemble.1, bf16[1,2,2,8,4096]{4,3,2,1,0:T(8,128)(2,1)} %perturb.1, f32[8,4096]{1,0:T(8,128)} %observed.1), custom_call_target="tpu_custom_call" | custom-call | tf_op jit(solution)/shard_map/filter_step/pallas_call | solution.py:317
  36.6 0.7 %copy.8 = f32[1,2,8,4096]{3,2,1,0:T(8,128)} copy(f32[1,2,8,4096]{3,2,1,0:T(8,128)S(1)} %filter_step.1) | data formatting | bytes 524288

commit v4 on v3

--- a/solution.py
+++ b/solution.py
@@ -15,7 +15,7 @@
 PLANES = 8
 PER_PLANE = 8
 BAND = COLS // PLANES
-PARTS = ((0, 4), (4, 4))
+PARTS = ((2, 2), (4, 2), (0, 2), (6, 2))
 COUPLE = (0.4, 0.6)
 DRAG = (0.0, 0.2)
 DT = 0.05
@@ -114,7 +114,7 @@
 
 def kernel(
     offspring_in, new_owner_in, nudge_in, ensemble, perturb, observed, out,
-    offspring, new_owner, nudge, noise, obs, tiles_a, tiles_b, picked_a, picked_b,
+    offspring, new_owner, nudge, noise, obs, tiles, picked,
     parent_row, parent_at,
     s_own, s_halo, s_outer, q_own, q_halo, q_outer, s1_own, s1_halo,
     target_own, target_halo, force_own, force_halo, pull_own, pull_halo,
@@ -124,7 +124,6 @@
     me, x = lax.axis_index("dom"), lax.axis_index("space")
     next_x, prev_x = lax.rem(x + 1, 4), lax.rem(x + 3, 4)
     plane, y, core = lax.div(me, 8), lax.rem(lax.div(me, 2), 4), lax.rem(me, 2)
-    tiles, picked = (tiles_a, tiles_b), (picked_a, picked_b)
     places = [
         (lax.rem(y + dy, 4) * 2 + lax.rem(core + dc, 2), lax.rem(y + dy, 4), lax.rem(core + dc, 2))
         for dy, dc in ((2, 1), (2, 0), (1, 1), (1, 0), (3, 1), (3, 0), (0, 1), (0, 0))
@@ -240,28 +239,37 @@
         rows = pl.ds(row, count)
         own_tiles[part].wait()
         tiles_of(part, MEMBERS - 1)(spread_recv.at[part])
-        for m in range(MEMBERS):
-            picked[part][m, rows] = tiles[part][parent_at[0, m], rows]
-
-        def deliver(to, layer, start, part=part, rows=rows):
-            pltpu.make_async_remote_copy(
-                src_ref=picked[part].at[to, rows],
-                dst_ref=s_own.at[core, rows, pl.ds(my_start, LANES)],
-                send_sem=deliver_send.at[part],
-                recv_sem=deliver_recv.at[part, plane],
-                device_id=(to, x),
-            ).start()
-
-        for_partners(deliver)
+
+        def one_plane(n, carry, part=part, rows=rows, count=PER_PLANE):
+            z = nth_plane(n)
+            for place in range(PER_PLANE):
+                m = z * PER_PLANE + place
+                picked[part][m, rows] = tiles[part][parent_at[0, m], rows]
+            for place, _, _ in places[:count]:
+                to = z * PER_PLANE + place
+                pltpu.make_async_remote_copy(
+                    src_ref=picked[part].at[to, rows],
+                    dst_ref=s_own.at[core, rows, pl.ds(my_start, LANES)],
+                    send_sem=deliver_send.at[part],
+                    recv_sem=deliver_recv.at[part, plane],
+                    device_id=(to, x),
+                ).start()
+            return carry
+
+        lax.fori_loop(0, PLANES - 1, one_plane, 0)
+        one_plane(PLANES - 1, 0, count=PER_PLANE - 1)
         s_own[core, rows, pl.ds(my_start, LANES)] = picked[part][me, rows]
 
     def forward(part, z):
         band = pl.ds(pl.multiple_of(z * BAND, BAND), BAND)
-        sides = (
-            ((low, s_halo, prev_x, 0), (pl.ds(2, 2), s_outer, next_x, 1)),
-            ((high, s_halo, next_x, 2), (pl.ds(4, 2), s_outer, prev_x, 3)),
-        )[part]
-        for rows, halo, to_x, number in sides:
+        row, count = PARTS[part]
+        rows = pl.ds(row, count)
+        sides = []
+        if row < 6:
+            sides.append((s_halo if row < 4 else s_outer, prev_x, 0))
+        if row >= 2:
+            sides.append((s_halo if row >= 4 else s_outer, next_x, 1))
+        for halo, to_x, number in sides:
             pltpu.make_async_remote_copy(
                 src_ref=s_own.at[:, rows, band],
                 dst_ref=halo.at[:, rows, band],
@@ -286,8 +294,8 @@
         tiles_of(part, MEMBERS - 1)(deliver_send.at[part])
     for one in early:
         one.wait()
-    for number, count in enumerate((4, 2, 4, 2)):
-        some = s_own.at[:, pl.ds(0, count)]
+    for number in range(2):
+        some = s_own.at[:, pl.ds(0, 6)]
         for sem in (row_recv, row_send):
             pltpu.make_async_copy(some, some, sem.at[number]).wait()
 
@@ -325,7 +333,8 @@
             pltpu.SMEM((ROWS,), F32),
             pltpu.VMEM((STEPS, 2, ROWS, COLS), jnp.bfloat16),
             pltpu.VMEM((ROWS, COLS), F32),
-            *[tiles] * 4,
+            [tiles] * len(PARTS),
+            [tiles] * len(PARTS),
             pltpu.VMEM((8, LANES), jnp.int32),
             pltpu.SMEM((8, LANES), jnp.int32),
             *[layers] * 10,
@@ -333,15 +342,15 @@
             forces,
             small,
             small,
-            dma((7,)),
+            dma((5 + len(PARTS),)),
+            dma((len(PARTS),)),
+            dma((len(PARTS),)),
+            dma((len(PARTS),)),
+            dma((len(PARTS), PLANES)),
+            dma((6,)),
+            dma((6,)),
             dma((2,)),
             dma((2,)),
-            dma((2,)),
-            dma((2, PLANES)),
-            dma((6,)),
-            dma((6,)),
-            dma((4,)),
-            dma((4,)),
         ],
         compiler_params=pltpu.CompilerParams(
             collective_id=0, has_side_effects=True, vmem_limit_bytes=48 * 1024 * 1024

time: 37.4 us -> 35.3 us (0.944)
  Pallas kernels: 36.6 us -> 34.6 us
    pallas_call x1, Pallas kernels: 36.6 us -> 34.6 us  [per_device(): pl.pallas_call(kernel, out_shape=pltpu.VMEM(ensemble.shape, F32), in_spec...]
where the time goes in v4:
time: 35.3 us
  Pallas kernels  34.6 us (98%)
  local copies, waits for them, and re-layouts  0.71 us (2%)
    pallas_call x1, Pallas kernels, per_device(): pl.pallas_call(kernel, out_shape=pltpu.VMEM(ensemble.shape, F32), in_spec...  34.6 us

profile of v4, /device:TPU:1, one launch (start us, length us, event | category | flops | bytes accessed | tf_op | source)
XLA Modules:
  0.0 35.3 jit_solution(9591170228797904132)
XLA Ops:
  0.0 34.6 %filter_step.1 = f32[1,2,8,4096]{3,2,1,0:T(8,128)S(1)} custom-call(s32[64]{0:T(128)} %offspring_in.1, s32[64]{0:T(128)} %new_owner_in.1, f32[8]{0:T(128)} %nudge_in.1, f32[1,2,8,4096]{3,2,1,0:T(8,128)} %ensemble.1, bf16[1,2,2,8,4096]{4,3,2,1,0:T(8,128)(2,1)} %perturb.1, f32[8,4096]{1,0:T(8,128)} %observed.1), custom_call_target="tpu_custom_call" | custom-call | tf_op jit(solution)/shard_map/filter_step/pallas_call | solution.py:325
  34.6 0.7 %copy.8 = f32[1,2,8,4096]{3,2,1,0:T(8,128)} copy(f32[1,2,8,4096]{3,2,1,0:T(8,128)S(1)} %filter_step.1) | data formatting | bytes 524288

commit v5 on v0

v5 whole, which is shorter than its diff:
```python
import jax
import jax.numpy as jnp
from jax import lax
from jax.experimental import pallas as pl
from jax.experimental.pallas import tpu as pltpu
from jax.sharding import PartitionSpec as P

STEPS = 2
COLS = 4096
ROWS = 8
SPACES = 4
MEMBERS = 64
LANES = 128
TILES = COLS // LANES
PLANES = 8
PER_PLANE = 8
BAND = TILES // PLANES
SPAN = 3 * ROWS
HALO = 6
SPREAD = ((2, 2), (4, 2), (0, 2), (6, 2))
DELIVER = (((2, 2),), ((4, 2),), ((0, 2),), ((6, 2),))
PARTS = [(spread, *rows) for spread, parts in enumerate(DELIVER) for rows in parts]
COUPLE = (0.4, 0.6)
DRAG = (0.0, 0.2)
DT = 0.05
BETA = 1.0
NOISE = 0.5
F32 = jnp.float32


def window(row, count=ROWS):
    return pl.ds(ROWS + row, count)


def shifted(ref, layer, row, by):
    turned = pltpu.roll(ref[layer, :, window(row), :], by % LANES, 2)
    lane = lax.broadcasted_iota(jnp.int32, turned.shape, 2)
    if by < 0:
        beside = jnp.concatenate([turned[1:], turned[:1]], axis=0)
        return jnp.where(lane == LANES - 1, beside, turned)
    beside = jnp.concatenate([turned[-1:], turned[:-1]], axis=0)
    return jnp.where(lane == 0, beside, turned)


def inside(x, row):
    if row == 0:
        return None
    at = lax.broadcasted_iota(jnp.int32, (TILES, ROWS, LANES), 1) + (x * ROWS + row)
    return (at >= 0) & (at < SPACES * ROWS)


def keep(value, mask):
    return value if mask is None else jnp.where(mask, value, 0.0)


def model_step(state, vort, slope, target, half, force, pull, x, step_no, last, out):
    for row in (-2, 2) if last else (-5, 3, 5):
        mask = inside(x, row)
        both = [state[layer, :, window(row), :] for layer in range(2)]
        for layer in range(2):
            left, right = shifted(state, layer, row, 1), shifted(state, layer, row, -1)
            above, below = (state[layer, :, window(row + by), :] for by in (-1, 1))
            value = (above + below) + (left + right) - (4.0 + COUPLE[layer]) * both[layer]
            value = value + COUPLE[layer] * both[1 - layer]
            vort[layer, :, window(row), :] = keep(value, mask)
            slope[layer, :, window(row), :] = right - left

    for row in (-1, 1) if last else (-4, 4):
        mask = inside(x, row)
        for layer in range(2):
            here, q = state[layer, :, window(row), :], vort[layer, :, window(row), :]
            ex_s = slope[layer, :, window(row), :]
            ex_q = shifted(vort, layer, row, -1) - shifted(vort, layer, row, 1)
            ny_s = state[layer, :, window(row + 1), :] - state[layer, :, window(row - 1), :]
            ny_q = vort[layer, :, window(row + 1), :] - vort[layer, :, window(row - 1), :]
            tendency = ny_s * ex_q - ex_s * (ny_q + 2.0 * BETA)
            change = (DT * 0.25) * tendency + force[step_no, layer, :, window(row), :]
            if DRAG[layer]:
                change = change - (DT * DRAG[layer]) * q
            if layer == 0:
                change = change - pull[window(row), :] * here
            target[layer, :, window(row), :] = q + change
            value = here - change * (1.0 / (4.0 + COUPLE[layer]))
            half[layer, :, window(row), :] = keep(value, mask)

    for row in (0,) if last else (-3, 3):
        mask = inside(x, row)
        both = [half[layer, :, window(row), :] for layer in range(2)]
        for layer in range(2):
            around = half[layer, :, window(row - 1), :] + half[layer, :, window(row + 1), :]
            around = around + shifted(half, layer, row, 1) + shifted(half, layer, row, -1)
            rest = around + COUPLE[layer] * both[1 - layer] - target[layer, :, window(row), :]
            value = rest * (1.0 / (4.0 + COUPLE[layer]))
            if last:
                for tile in range(TILES):
                    out[0, layer, :, pl.ds(tile * LANES, LANES)] = value[tile]
            else:
                state[layer, :, window(row), :] = keep(value, mask)


def kernel(
    offspring_in, new_owner_in, nudge_in, ensemble, perturb, observed, out,
    offspring, new_owner, nudge, noise, obs, tiles, picked, parent_row, parent_at,
    state, vort, slope, target, half, force, pull,
    local_sem, spread_send, spread_recv, deliver_send, deliver_recv,
    early_send, early_recv, row_send, row_recv,
):
    me, x = lax.axis_index("dom"), lax.axis_index("space")
    plane, y, core = lax.div(me, 8), lax.rem(lax.div(me, 2), 4), lax.rem(me, 2)
    my_tile = lax.div(me, 2)
    places = [
        (lax.rem(y + dy, 4), lax.rem(core + dc, 2))
        for dy, dc in ((2, 1), (2, 0), (1, 1), (1, 0), (3, 1), (3, 0), (0, 1), (0, 0))
    ]

    def nth_plane(n):
        far = (n + 1) // 2
        return lax.rem(plane + jnp.where(n % 2 == 1, 4 - far, 4 + far), PLANES)

    def each_plane(act):
        def one_plane(n, carry):
            act(nth_plane(n), PER_PLANE)
            return carry

        lax.fori_loop(0, PLANES - 1, one_plane, 0)
        act(plane, PER_PLANE - 1)

    def each_partner(act):
        def in_plane(z, count):
            for at_y, at_core in places[:count]:
                act(z * PER_PLANE + at_y * 2 + at_core, z, at_y, at_core)

        each_plane(in_plane)

    loads = [
        pltpu.make_async_copy(new_owner_in, new_owner, local_sem.at[0]),
        pltpu.make_async_copy(offspring_in, offspring, local_sem.at[1]),
        pltpu.make_async_copy(nudge_in, nudge, local_sem.at[2]),
        pltpu.make_async_copy(perturb.at[0], noise, local_sem.at[3]),
        pltpu.make_async_copy(observed, obs, local_sem.at[4]),
    ]
    for load in loads:
        load.start()

    barrier = pltpu.get_barrier_semaphore()
    each_partner(lambda to, *_: pl.semaphore_signal(barrier, inc=1, device_id=(to, x)))

    has_prev, has_next = x > 0, x < SPACES - 1

    @pl.when(has_prev)
    def _():
        pl.semaphore_signal(barrier, inc=1, device_id=(me, x - 1))

    @pl.when(has_next)
    def _():
        pl.semaphore_signal(barrier, inc=1, device_id=(me, x + 1))

    beside = jnp.where(has_prev, 1, 0) + jnp.where(has_next, 1, 0)
    pl.semaphore_wait(barrier, MEMBERS - 1 + beside)

    own_tiles = []
    for part, (row, count) in enumerate(SPREAD):
        rows = pl.ds(row, count)

        def spread_to(to, z, at_y, at_core, part=part, rows=rows):
            start = pl.multiple_of((z * 4 + at_y) * LANES, LANES)
            pltpu.make_async_remote_copy(
                src_ref=ensemble.at[0, at_core, rows, pl.ds(start, LANES)],
                dst_ref=tiles[part].at[me, rows],
                send_sem=spread_send.at[part],
                recv_sem=spread_recv.at[part],
                device_id=(to, x),
            ).start()

        each_partner(spread_to)
        start = pl.multiple_of(my_tile * LANES, LANES)
        own = pltpu.make_async_copy(
            ensemble.at[0, core, rows, pl.ds(start, LANES)],
            tiles[part].at[me, rows],
            local_sem.at[5 + part],
        )
        own.start()
        own_tiles.append(own)

    for load in loads:
        load.wait()
    lane = lax.broadcasted_iota(jnp.int32, (8, LANES), 1)
    copy = jnp.zeros((8, LANES), jnp.int32)
    for j in range(MEMBERS):
        copy = jnp.where(lane == new_owner[j], j, copy)
    parent, total = jnp.zeros((8, LANES), jnp.int32), jnp.int32(0)
    for i in range(MEMBERS):
        total = total + offspring[i]
        parent = parent + (total <= copy).astype(jnp.int32)
    parent_row[...] = jnp.minimum(parent, MEMBERS - 1)
    to_scalars = pltpu.make_async_copy(parent_row, parent_at, local_sem.at[0])
    to_scalars.start()

    at = lax.broadcasted_iota(jnp.int32, (ROWS, LANES), 0)
    rate = jnp.zeros((ROWS, LANES), F32)
    for r in range(ROWS):
        rate = jnp.where(at == r, DT * nudge[r], rate)
    own_rows = window(0)
    pull[own_rows, :] = rate
    for tile in range(TILES):
        here = pl.ds(tile * LANES, LANES)
        drawn = rate * obs[:, here]
        for t in range(STEPS):
            for layer in range(2):
                value = NOISE * noise[t, layer, :, here].astype(F32)
                force[t, layer, tile, own_rows, :] = value + drawn if layer == 0 else value

    def row_copy(src, dst, send, recv, to_x):
        return pltpu.make_async_remote_copy(
            src_ref=src, dst_ref=dst, send_sem=send, recv_sem=recv, device_id=(me, to_x)
        )

    def early_copies(side):
        copies = []
        by, to_x = ((ROWS, x - 1), (-ROWS, x + 1))[side]
        for number, (row, count) in enumerate((((0, 4), (0, 1)), ((4, 4), (7, 1)))[side]):
            src, dst = window(row, count), window(row + by, count)
            copies.append((force.at[number, :, :, src, :], force.at[number, :, :, dst, :]))
            if number == 0:
                copies.append((pull.at[src, :], pull.at[dst, :]))
        return [
            row_copy(src, dst, early_send.at[side, n], early_recv.at[side, n], to_x)
            for n, (src, dst) in enumerate(copies)
        ]

    @pl.when(has_prev)
    def _():
        for one in early_copies(0):
            one.start()

    @pl.when(has_next)
    def _():
        for one in early_copies(1):
            one.start()

    to_scalars.wait()

    def tiles_of(row, count, number):
        some = tiles[0].at[pl.ds(0, number), pl.ds(row, count)]
        return lambda sem: pltpu.make_async_copy(some, some, sem).wait()

    arrived = -1
    for part, (spread, row, count) in enumerate(PARTS):
        if spread > arrived:
            arrived = spread
            own_tiles[spread].wait()
            tiles_of(*SPREAD[spread], MEMBERS - 1)(spread_recv.at[spread])
        rows, lands = pl.ds(row, count), window(row, count)

        def deliver_in(z, count, part=part, spread=spread, rows=rows, lands=lands):
            for place in range(PER_PLANE):
                m = z * PER_PLANE + place
                picked[part][m, rows] = tiles[spread][parent_at[0, m], rows]
            for at_y, at_core in places[:count]:
                to = z * PER_PLANE + at_y * 2 + at_core
                pltpu.make_async_remote_copy(
                    src_ref=picked[part].at[to, rows],
                    dst_ref=state.at[core, my_tile, lands, :],
                    send_sem=deliver_send.at[part],
                    recv_sem=deliver_recv.at[part, plane],
                    device_id=(to, x),
                ).start()

        each_plane(deliver_in)
        state[core, my_tile, lands, :] = picked[part][me, rows]

    for part, (_, row, count) in enumerate(PARTS):

        def pass_on(z, number, part=part, row=row, count=count):
            tiles_of(row, count, number)(deliver_recv.at[part, z])
            band = pl.ds(z * BAND, BAND)
            for side, (by, to_x, there) in enumerate(
                ((ROWS, x - 1, has_prev), (-ROWS, x + 1, has_next))
            ):
                if row < HALO if side == 0 else row >= ROWS - HALO:

                    @pl.when(there)
                    def _(side=side, by=by, to_x=to_x):
                        row_copy(
                            state.at[:, band, window(row, count), :],
                            state.at[:, band, window(row + by, count), :],
                            row_send.at[side],
                            row_recv.at[side],
                            to_x,
                        ).start()

        each_plane(pass_on)

    for part, rows in enumerate(SPREAD):
        tiles_of(*rows, MEMBERS - 1)(spread_send.at[part])
    for part, (_, *rows) in enumerate(PARTS):
        tiles_of(*rows, MEMBERS - 1)(deliver_send.at[part])

    some = state.at[:, :, window(0, HALO), :]
    for side, (there, row) in enumerate(((has_prev, -HALO), (has_next, ROWS))):

        @pl.when(there)
        def _(side=side):
            for one in early_copies(side):
                one.wait_send()
            for one in early_copies(1 - side):
                one.wait_recv()
            pltpu.make_async_copy(some, some, row_send.at[side]).wait()
            pltpu.make_async_copy(some, some, row_recv.at[1 - side]).wait()

        @pl.when(jnp.logical_not(there))
        def _(row=row):
            state[:, :, window(row, HALO), :] = jnp.zeros((2, TILES, HALO, LANES), F32)

    for t in range(STEPS):
        model_step(state, vort, slope, target, half, force, pull, x, t, t == STEPS - 1, out)


def per_device(ensemble, offspring, new_owner, perturb, observed, nudge_rate):
    field = pltpu.VMEM((2, TILES, SPAN, LANES), F32)
    tiles = pltpu.VMEM((MEMBERS, 8, LANES), F32)
    dma = pltpu.SemaphoreType.DMA
    operands = [
        pltpu.with_memory_space_constraint(a, pltpu.HBM)
        for a in (offspring, new_owner, nudge_rate, ensemble, perturb, observed)
    ]
    return pl.pallas_call(
        kernel,
        out_shape=pltpu.VMEM(ensemble.shape, F32),
        in_specs=[pl.BlockSpec(memory_space=pltpu.HBM)] * 6,
        out_specs=pl.BlockSpec(memory_space=pltpu.VMEM),
        scratch_shapes=[
            pltpu.SMEM((MEMBERS,), jnp.int32),
            pltpu.SMEM((MEMBERS,), jnp.int32),
            pltpu.SMEM((ROWS,), F32),
            pltpu.VMEM((STEPS, 2, ROWS, COLS), jnp.bfloat16),
            pltpu.VMEM((ROWS, COLS), F32),
            [tiles] * len(SPREAD),
            [tiles] * len(PARTS),
            pltpu.VMEM((8, LANES), jnp.int32),
            pltpu.SMEM((8, LANES), jnp.int32),
            *[field] * 5,
            pltpu.VMEM((STEPS, 2, TILES, SPAN, LANES), F32),
            pltpu.VMEM((SPAN, LANES), F32),
            dma((5 + len(SPREAD),)),
            dma((len(SPREAD),)),
            dma((len(SPREAD),)),
            dma((len(PARTS),)),
            dma((len(PARTS), PLANES)),
            dma((2, 3)),
            dma((2, 3)),
            dma((2,)),
            dma((2,)),
        ],
        compiler_params=pltpu.CompilerParams(
            collective_id=0, has_side_effects=True, vmem_limit_bytes=48 * 1024 * 1024
        ),
        name="filter_step",
    )(*operands)


def solution(mesh):
    in_specs = (
        P("dom", None, "space", None),
        P(),
        P(),
        P("dom", None, None, "space", None),
        P("space", None),
        P("space"),
    )
    out_specs = P("dom", None, "space", None)
    return jax.shard_map(
        per_device, mesh=mesh, in_specs=in_specs, out_specs=out_specs, check_vma=False
    )
```

time: 167 us -> 32.7 us (0.20)
  the two profiles are of different devices: /device:TPU:6 before, /device:TPU:1 now
where the time goes in v5:
time: 32.7 us; the launch traced here: 32.6 us
  Pallas kernels  31.9 us (98%)
  local copies, waits for them, and re-layouts  0.71 us (2%)
    pallas_call x1, Pallas kernels, per_device(): pl.pallas_call(kernel, out_shape=pltpu.VMEM(ensemble.shape, F32), in_spec...  31.9 us
    unnamed x1, local copies, waits for them, and re-layouts  0.71 us

profile of v5, /device:TPU:1, one launch (start us, length us, event | category | flops | bytes accessed | tf_op | source)
XLA Modules:
  0.0 32.6 jit_solution(923912474665982145)
XLA Ops:
  0.0 31.9 %filter_step.1 = f32[1,2,8,4096]{3,2,1,0:T(8,128)S(1)} custom-call(s32[64]{0:T(128)} %offspring_in.1, s32[64]{0:T(128)} %new_owner_in.1, f32[8]{0:T(128)} %nudge_in.1, f32[1,2,8,4096]{3,2,1,0:T(8,128)} %ensemble.1, bf16[1,2,2,8,4096]{4,3,2,1,0:T(8,128)(2,1)} %perturb.1, f32[8,4096]{1,0:T(8,128)} %observed.1), custom_call_target="tpu_custom_call" | custom-call | tf_op jit(solution)/shard_map/filter_step/pallas_call | solution.py:327
  31.9 0.7 %copy.8 = f32[1,2,8,4096]{3,2,1,0:T(8,128)} copy(f32[1,2,8,4096]{3,2,1,0:T(8,128)S(1)} %filter_step.1) | data formatting | bytes 524288

commit v6 on v5

--- a/solution.py
+++ b/solution.py
@@ -20,6 +20,7 @@
 SPREAD = ((2, 2), (4, 2), (0, 2), (6, 2))
 DELIVER = (((2, 2),), ((4, 2),), ((0, 2),), ((6, 2),))
 PARTS = [(spread, *rows) for spread, parts in enumerate(DELIVER) for rows in parts]
+DIRECT = (2, 3)
 COUPLE = (0.4, 0.6)
 DRAG = (0.0, 0.2)
 DT = 0.05
@@ -103,7 +104,7 @@
     offspring, new_owner, nudge, noise, obs, tiles, picked, parent_row, parent_at,
     state, vort, slope, target, half, force, pull,
     local_sem, spread_send, spread_recv, deliver_send, deliver_recv,
-    early_send, early_recv, row_send, row_recv,
+    early_send, early_recv, row_send, row_recv, direct_send, direct_recv,
 ):
     me, x = lax.axis_index("dom"), lax.axis_index("space")
     plane, y, core = lax.div(me, 8), lax.rem(lax.div(me, 2), 4), lax.rem(me, 2)
@@ -244,6 +245,10 @@
         some = tiles[0].at[pl.ds(0, number), pl.ds(row, count)]
         return lambda sem: pltpu.make_async_copy(some, some, sem).wait()
 
+    def sides_of(row):
+        sides = ((0, (ROWS, x - 1, has_prev)), (1, (-ROWS, x + 1, has_next)))
+        return [sides[n] for n in (0, 1) if (row >= ROWS - HALO if n else row < HALO)]
+
     arrived = -1
     for part, (spread, row, count) in enumerate(PARTS):
         if spread > arrived:
@@ -252,7 +257,9 @@
             tiles_of(*SPREAD[spread], MEMBERS - 1)(spread_recv.at[spread])
         rows, lands = pl.ds(row, count), window(row, count)
 
-        def deliver_in(z, count, part=part, spread=spread, rows=rows, lands=lands):
+        def deliver_in(
+            z, count, part=part, spread=spread, row=row, size=count, rows=rows, lands=lands
+        ):
             for place in range(PER_PLANE):
                 m = z * PER_PLANE + place
                 picked[part][m, rows] = tiles[spread][parent_at[0, m], rows]
@@ -265,6 +272,20 @@
                     recv_sem=deliver_recv.at[part, plane],
                     device_id=(to, x),
                 ).start()
+            if part in DIRECT:
+                for side, (by, to_x, there) in sides_of(row):
+
+                    @pl.when(there)
+                    def _(side=side, by=by, to_x=to_x):
+                        for at_y, at_core in places:
+                            to = z * PER_PLANE + at_y * 2 + at_core
+                            pltpu.make_async_remote_copy(
+                                src_ref=picked[part].at[to, rows],
+                                dst_ref=state.at[core, my_tile, window(row + by, size), :],
+                                send_sem=direct_send.at[part],
+                                recv_sem=direct_recv.at[part],
+                                device_id=(to, to_x),
+                            ).start()
 
         each_plane(deliver_in)
         state[core, my_tile, lands, :] = picked[part][me, rows]
@@ -274,10 +295,8 @@
         def pass_on(z, number, part=part, row=row, count=count):
             tiles_of(row, count, number)(deliver_recv.at[part, z])
             band = pl.ds(z * BAND, BAND)
-            for side, (by, to_x, there) in enumerate(
-                ((ROWS, x - 1, has_prev), (-ROWS, x + 1, has_next))
-            ):
-                if row < HALO if side == 0 else row >= ROWS - HALO:
+            for side, (by, to_x, there) in sides_of(row):
+                if part not in DIRECT:
 
                     @pl.when(there)
                     def _(side=side, by=by, to_x=to_x):
@@ -296,7 +315,10 @@
     for part, (_, *rows) in enumerate(PARTS):
         tiles_of(*rows, MEMBERS - 1)(deliver_send.at[part])
 
-    some = state.at[:, :, window(0, HALO), :]
+    passed = [
+        sum(n for part, (_, r, n) in enumerate(PARTS) if part not in DIRECT and (r >= ROWS - HALO if side else r < HALO))
+        for side in (0, 1)
+    ]
     for side, (there, row) in enumerate(((has_prev, -HALO), (has_next, ROWS))):
 
         @pl.when(there)
@@ -305,8 +327,16 @@
                 one.wait_send()
             for one in early_copies(1 - side):
                 one.wait_recv()
-            pltpu.make_async_copy(some, some, row_send.at[side]).wait()
-            pltpu.make_async_copy(some, some, row_recv.at[1 - side]).wait()
+            gone = state.at[:, :, window(0, passed[side]), :]
+            came = state.at[:, :, window(0, passed[1 - side]), :]
+            pltpu.make_async_copy(gone, gone, row_send.at[side]).wait()
+            pltpu.make_async_copy(came, came, row_recv.at[1 - side]).wait()
+            for part in DIRECT:
+                _, row, count = PARTS[part]
+                if side in [n for n, _ in sides_of(row)]:
+                    tiles_of(row, count, MEMBERS)(direct_send.at[part])
+                else:
+                    tiles_of(row, count, MEMBERS)(direct_recv.at[part])
 
         @pl.when(jnp.logical_not(there))
         def _(row=row):
@@ -351,6 +381,8 @@
             dma((2, 3)),
             dma((2,)),
             dma((2,)),
+            dma((len(PARTS),)),
+            dma((len(PARTS),)),
         ],
         compiler_params=pltpu.CompilerParams(
             collective_id=0, has_side_effects=True, vmem_limit_bytes=48 * 1024 * 1024

time: 32.7 us -> 32.3 us (0.988); the launches traced: 32.6 us -> 31.8 us
  Pallas kernels: 31.9 us -> 31.1 us
    pallas_call x1, Pallas kernels: 31.9 us -> 31.1 us  [per_device(): pl.pallas_call(kernel, out_shape=pltpu.VMEM(ensemble.shape, F32), in_spec...]
where the time goes in v6:
time: 32.3 us; the launch traced here: 31.8 us
  Pallas kernels  31.1 us (96%)
  local copies, waits for them, and re-layouts  0.71 us (2%)
    pallas_call x1, Pallas kernels, per_device(): pl.pallas_call(kernel, out_shape=pltpu.VMEM(ensemble.shape, F32), in_spec...  31.1 us
    unnamed x1, local copies, waits for them, and re-layouts  0.71 us

profile of v6, /device:TPU:1, one launch (start us, length us, event | category | flops | bytes accessed | tf_op | source)
XLA Modules:
  0.0 31.8 jit_solution(1351564563937716280)
XLA Ops:
  0.0 31.1 %filter_step.1 = f32[1,2,8,4096]{3,2,1,0:T(8,128)S(1)} custom-call(s32[64]{0:T(128)} %offspring_in.1, s32[64]{0:T(128)} %new_owner_in.1, f32[8]{0:T(128)} %nudge_in.1, f32[1,2,8,4096]{3,2,1,0:T(8,128)} %ensemble.1, bf16[1,2,2,8,4096]{4,3,2,1,0:T(8,128)(2,1)} %perturb.1, f32[8,4096]{1,0:T(8,128)} %observed.1), custom_call_target="tpu_custom_call" | custom-call | tf_op jit(solution)/shard_map/filter_step/pallas_call | solution.py:357
  31.1 0.7 %copy.8 = f32[1,2,8,4096]{3,2,1,0:T(8,128)} copy(f32[1,2,8,4096]{3,2,1,0:T(8,128)S(1)} %filter_step.1) | data formatting | bytes 524288

commit v7 on v6

--- a/solution.py
+++ b/solution.py
@@ -33,8 +33,8 @@
     return pl.ds(ROWS + row, count)
 
 
-def shifted(ref, layer, row, by):
-    turned = pltpu.roll(ref[layer, :, window(row), :], by % LANES, 2)
+def shifted(ref, layer, row, by, count=ROWS):
+    turned = pltpu.roll(ref[layer, :, window(row, count), :], by % LANES, 2)
     lane = lax.broadcasted_iota(jnp.int32, turned.shape, 2)
     if by < 0:
         beside = jnp.concatenate([turned[1:], turned[:1]], axis=0)
@@ -43,60 +43,53 @@
     return jnp.where(lane == 0, beside, turned)
 
 
-def inside(x, row):
-    if row == 0:
-        return None
-    at = lax.broadcasted_iota(jnp.int32, (TILES, ROWS, LANES), 1) + (x * ROWS + row)
-    return (at >= 0) & (at < SPACES * ROWS)
-
-
-def keep(value, mask):
-    return value if mask is None else jnp.where(mask, value, 0.0)
-
-
-def model_step(state, vort, slope, target, half, force, pull, x, step_no, last, out):
-    for row in (-2, 2) if last else (-5, 3, 5):
-        mask = inside(x, row)
-        both = [state[layer, :, window(row), :] for layer in range(2)]
-        for layer in range(2):
-            left, right = shifted(state, layer, row, 1), shifted(state, layer, row, -1)
-            above, below = (state[layer, :, window(row + by), :] for by in (-1, 1))
-            value = (above + below) + (left + right) - (4.0 + COUPLE[layer]) * both[layer]
-            value = value + COUPLE[layer] * both[1 - layer]
-            vort[layer, :, window(row), :] = keep(value, mask)
-            slope[layer, :, window(row), :] = right - left
-
-    for row in (-1, 1) if last else (-4, 4):
-        mask = inside(x, row)
-        for layer in range(2):
-            here, q = state[layer, :, window(row), :], vort[layer, :, window(row), :]
-            ex_s = slope[layer, :, window(row), :]
-            ex_q = shifted(vort, layer, row, -1) - shifted(vort, layer, row, 1)
-            ny_s = state[layer, :, window(row + 1), :] - state[layer, :, window(row - 1), :]
-            ny_q = vort[layer, :, window(row + 1), :] - vort[layer, :, window(row - 1), :]
-            tendency = ny_s * ex_q - ex_s * (ny_q + 2.0 * BETA)
-            change = (DT * 0.25) * tendency + force[step_no, layer, :, window(row), :]
-            if DRAG[layer]:
-                change = change - (DT * DRAG[layer]) * q
-            if layer == 0:
-                change = change - pull[window(row), :] * here
-            target[layer, :, window(row), :] = q + change
-            value = here - change * (1.0 / (4.0 + COUPLE[layer]))
-            half[layer, :, window(row), :] = keep(value, mask)
-
-    for row in (0,) if last else (-3, 3):
-        mask = inside(x, row)
-        both = [half[layer, :, window(row), :] for layer in range(2)]
-        for layer in range(2):
-            around = half[layer, :, window(row - 1), :] + half[layer, :, window(row + 1), :]
-            around = around + shifted(half, layer, row, 1) + shifted(half, layer, row, -1)
-            rest = around + COUPLE[layer] * both[1 - layer] - target[layer, :, window(row), :]
-            value = rest * (1.0 / (4.0 + COUPLE[layer]))
-            if last:
-                for tile in range(TILES):
-                    out[0, layer, :, pl.ds(tile * LANES, LANES)] = value[tile]
-            else:
-                state[layer, :, window(row), :] = keep(value, mask)
+def keep(value, x, row):
+    if row >= 0 and row + value.shape[1] <= ROWS:
+        return value
+    at = lax.broadcasted_iota(jnp.int32, value.shape, 1) + (x * ROWS + row)
+    return jnp.where((at >= 0) & (at < SPACES * ROWS), value, 0.0)
+
+
+def potential(state, vort, slope, x, row, count=ROWS):
+    rows = window(row, count)
+    both = [state[layer, :, rows, :] for layer in range(2)]
+    for layer in range(2):
+        left, right = (shifted(state, layer, row, by, count) for by in (1, -1))
+        above, below = (state[layer, :, window(row + by, count), :] for by in (-1, 1))
+        value = (above + below) + (left + right) - (4.0 + COUPLE[layer]) * both[layer]
+        value = value + COUPLE[layer] * both[1 - layer]
+        vort[layer, :, rows, :] = keep(value, x, row)
+        slope[layer, :, rows, :] = right - left
+
+
+def first_sweep(state, vort, slope, target, half, force, pull, x, step_no, row):
+    rows = window(row)
+    for layer in range(2):
+        here, q, ex_s = (ref[layer, :, rows, :] for ref in (state, vort, slope))
+        ex_q = shifted(vort, layer, row, -1) - shifted(vort, layer, row, 1)
+        ny_s, ny_q = (
+            ref[layer, :, window(row + 1), :] - ref[layer, :, window(row - 1), :]
+            for ref in (state, vort)
+        )
+        tendency = ny_s * ex_q - ex_s * (ny_q + 2.0 * BETA)
+        change = (DT * 0.25) * tendency + force[step_no, layer, :, rows, :]
+        if DRAG[layer]:
+            change = change - (DT * DRAG[layer]) * q
+        if layer == 0:
+            change = change - pull[rows, :] * here
+        target[layer, :, rows, :] = q + change
+        value = here - change * (1.0 / (4.0 + COUPLE[layer]))
+        half[layer, :, rows, :] = keep(value, x, row)
+
+
+def second_sweep(half, target, x, row, put):
+    rows = window(row)
+    both = [half[layer, :, rows, :] for layer in range(2)]
+    for layer in range(2):
+        around = half[layer, :, window(row - 1), :] + half[layer, :, window(row + 1), :]
+        around = around + shifted(half, layer, row, 1) + shifted(half, layer, row, -1)
+        rest = around + COUPLE[layer] * both[1 - layer] - target[layer, :, rows, :]
+        put(layer, keep(rest * (1.0 / (4.0 + COUPLE[layer])), x, row))
 
 
 def kernel(
@@ -140,22 +133,21 @@
         pltpu.make_async_copy(perturb.at[0], noise, local_sem.at[3]),
         pltpu.make_async_copy(observed, obs, local_sem.at[4]),
     ]
+    barrier = pltpu.get_barrier_semaphore()
+    each_partner(lambda to, *_: pl.semaphore_signal(barrier, inc=1, device_id=(to, x)))
+
+    has_prev, has_next = x > 0, x < SPACES - 1
+
+    @pl.when(has_prev)
+    def _():
+        pl.semaphore_signal(barrier, inc=1, device_id=(me, x - 1))
+
+    @pl.when(has_next)
+    def _():
+        pl.semaphore_signal(barrier, inc=1, device_id=(me, x + 1))
+
     for load in loads:
         load.start()
-
-    barrier = pltpu.get_barrier_semaphore()
-    each_partner(lambda to, *_: pl.semaphore_signal(barrier, inc=1, device_id=(to, x)))
-
-    has_prev, has_next = x > 0, x < SPACES - 1
-
-    @pl.when(has_prev)
-    def _():
-        pl.semaphore_signal(barrier, inc=1, device_id=(me, x - 1))
-
-    @pl.when(has_next)
-    def _():
-        pl.semaphore_signal(barrier, inc=1, device_id=(me, x + 1))
-
     beside = jnp.where(has_prev, 1, 0) + jnp.where(has_next, 1, 0)
     pl.semaphore_wait(barrier, MEMBERS - 1 + beside)
 
@@ -310,40 +302,94 @@
 
         each_plane(pass_on)
 
+    passed = [
+        sum(
+            count
+            for part, (_, row, count) in enumerate(PARTS)
+            if part not in DIRECT and (row >= ROWS - HALO if side else row < HALO)
+        )
+        for side in (0, 1)
+    ]
+
+    def some_rows(side, sem):
+        some = state.at[:, :, window(0, passed[side]), :]
+        return pltpu.make_async_copy(some, some, sem.at[side])
+
+    def direct_parts(side):
+        return [p for p in DIRECT if side in [n for n, _ in sides_of(PARTS[p][1])]]
+
+    def rows_from(side):
+        for one in early_copies(side):
+            one.wait_recv()
+        some_rows(side, row_recv).wait()
+        for part in direct_parts(side):
+            tiles_of(*PARTS[part][1:], MEMBERS)(direct_recv.at[part])
+
+    def no_rows(row):
+        state[:, :, window(row, HALO), :] = jnp.zeros((2, TILES, HALO, LANES), F32)
+
+    def one_side(q_row, s_row):
+        potential(state, vort, slope, x, q_row)
+        first_sweep(state, vort, slope, target, half, force, pull, x, 0, s_row)
+
+    potential(state, vort, slope, x, 1, ROWS - 2)
+
+    @pl.when(jnp.logical_not(has_prev))
+    def _():
+        no_rows(-HALO)
+        one_side(-5, -4)
+
+    @pl.when(has_next)
+    def _():
+        rows_from(0)
+
+    @pl.when(jnp.logical_not(has_next))
+    def _():
+        no_rows(ROWS)
+
+    one_side(5, 4)
+
+    @pl.when(has_prev)
+    def _():
+        rows_from(1)
+        one_side(-5, -4)
+
+    for side, there in enumerate((has_prev, has_next)):
+
+        @pl.when(there)
+        def _(side=side):
+            some_rows(side, row_send).wait()
+
+    for row in (-3, 3):
+
+        def put_state(layer, value, row=row):
+            state[layer, :, window(row), :] = value
+
+        second_sweep(half, target, x, row, put_state)
+
+    for row in (-2, 2):
+        potential(state, vort, slope, x, row)
+    for row in (-1, 1):
+        first_sweep(state, vort, slope, target, half, force, pull, x, 1, row)
+
+    def put_out(layer, value):
+        for tile in range(TILES):
+            out[0, layer, :, pl.ds(tile * LANES, LANES)] = value[tile]
+
+    second_sweep(half, target, x, 0, put_out)
+
     for part, rows in enumerate(SPREAD):
         tiles_of(*rows, MEMBERS - 1)(spread_send.at[part])
     for part, (_, *rows) in enumerate(PARTS):
         tiles_of(*rows, MEMBERS - 1)(deliver_send.at[part])
-
-    passed = [
-        sum(n for part, (_, r, n) in enumerate(PARTS) if part not in DIRECT and (r >= ROWS - HALO if side else r < HALO))
-        for side in (0, 1)
-    ]
-    for side, (there, row) in enumerate(((has_prev, -HALO), (has_next, ROWS))):
+    for side, there in enumerate((has_prev, has_next)):
 
         @pl.when(there)
         def _(side=side):
             for one in early_copies(side):
                 one.wait_send()
-            for one in early_copies(1 - side):
-                one.wait_recv()
-            gone = state.at[:, :, window(0, passed[side]), :]
-            came = state.at[:, :, window(0, passed[1 - side]), :]
-            pltpu.make_async_copy(gone, gone, row_send.at[side]).wait()
-            pltpu.make_async_copy(came, came, row_recv.at[1 - side]).wait()
-            for part in DIRECT:
-                _, row, count = PARTS[part]
-                if side in [n for n, _ in sides_of(row)]:
-                    tiles_of(row, count, MEMBERS)(direct_send.at[part])
-                else:
-                    tiles_of(row, count, MEMBERS)(direct_recv.at[part])
-
-        @pl.when(jnp.logical_not(there))
-        def _(row=row):
-            state[:, :, window(row, HALO), :] = jnp.zeros((2, TILES, HALO, LANES), F32)
-
-    for t in range(STEPS):
-        model_step(state, vort, slope, target, half, force, pull, x, t, t == STEPS - 1, out)
+            for part in direct_parts(side):
+                tiles_of(*PARTS[part][1:], MEMBERS)(direct_send.at[part])
 
 
 def per_device(ensemble, offspring, new_owner, perturb, observed, nudge_rate):

time: 32.3 us -> 32 us (level)
  no operation moved by 1% of the time
where the time goes in v7:
time: 32 us; the launch traced here: 31.5 us
  Pallas kernels  30.8 us (96%)
  local copies, waits for them, and re-layouts  0.71 us (2%)
    pallas_call x1, Pallas kernels, per_device(): pl.pallas_call(kernel, out_shape=pltpu.VMEM(ensemble.shape, F32), in_spec...  30.8 us
    unnamed x1, local copies, waits for them, and re-layouts  0.71 us

profile of v7, /device:TPU:1, one launch (start us, length us, event | category | flops | bytes accessed | tf_op | source)
XLA Modules:
  0.0 31.5 jit_solution(4355011657117532588)
XLA Ops:
  0.0 30.8 %filter_step.1 = f32[1,2,8,4096]{3,2,1,0:T(8,128)S(1)} custom-call(s32[64]{0:T(128)} %offspring_in.1, s32[64]{0:T(128)} %new_owner_in.1, f32[8]{0:T(128)} %nudge_in.1, f32[1,2,8,4096]{3,2,1,0:T(8,128)} %ensemble.1, bf16[1,2,2,8,4096]{4,3,2,1,0:T(8,128)(2,1)} %perturb.1, f32[8,4096]{1,0:T(8,128)} %observed.1), custom_call_target="tpu_custom_call" | custom-call | tf_op jit(solution)/shard_map/filter_step/pallas_call | solution.py:403
  30.8 0.7 %copy.8 = f32[1,2,8,4096]{3,2,1,0:T(8,128)} copy(f32[1,2,8,4096]{3,2,1,0:T(8,128)S(1)} %filter_step.1) | data formatting | bytes 524288

commit v8 on v7

--- a/solution.py
+++ b/solution.py
@@ -137,14 +137,15 @@
     each_partner(lambda to, *_: pl.semaphore_signal(barrier, inc=1, device_id=(to, x)))
 
     has_prev, has_next = x > 0, x < SPACES - 1
+    prev_x, next_x = jnp.maximum(x - 1, 0), jnp.minimum(x + 1, SPACES - 1)
 
     @pl.when(has_prev)
     def _():
-        pl.semaphore_signal(barrier, inc=1, device_id=(me, x - 1))
+        pl.semaphore_signal(barrier, inc=1, device_id=(me, prev_x))
 
     @pl.when(has_next)
     def _():
-        pl.semaphore_signal(barrier, inc=1, device_id=(me, x + 1))
+        pl.semaphore_signal(barrier, inc=1, device_id=(me, next_x))
 
     for load in loads:
         load.start()
@@ -210,7 +211,7 @@
 
     def early_copies(side):
         copies = []
-        by, to_x = ((ROWS, x - 1), (-ROWS, x + 1))[side]
+        by, to_x = ((ROWS, prev_x), (-ROWS, next_x))[side]
         for number, (row, count) in enumerate((((0, 4), (0, 1)), ((4, 4), (7, 1)))[side]):
             src, dst = window(row, count), window(row + by, count)
             copies.append((force.at[number, :, :, src, :], force.at[number, :, :, dst, :]))
@@ -238,7 +239,7 @@
         return lambda sem: pltpu.make_async_copy(some, some, sem).wait()
 
     def sides_of(row):
-        sides = ((0, (ROWS, x - 1, has_prev)), (1, (-ROWS, x + 1, has_next)))
+        sides = ((0, (ROWS, prev_x, has_prev)), (1, (-ROWS, next_x, has_next)))
         return [sides[n] for n in (0, 1) if (row >= ROWS - HALO if n else row < HALO)]
 
     arrived = -1
@@ -261,7 +262,7 @@
                     src_ref=picked[part].at[to, rows],
                     dst_ref=state.at[core, my_tile, lands, :],
                     send_sem=deliver_send.at[part],
-                    recv_sem=deliver_recv.at[part, plane],
+                    recv_sem=deliver_recv.at[part, 0 if part in DIRECT else plane],
                     device_id=(to, x),
                 ).start()
             if part in DIRECT:
@@ -288,19 +289,21 @@
             tiles_of(row, count, number)(deliver_recv.at[part, z])
             band = pl.ds(z * BAND, BAND)
             for side, (by, to_x, there) in sides_of(row):
-                if part not in DIRECT:
-
-                    @pl.when(there)
-                    def _(side=side, by=by, to_x=to_x):
-                        row_copy(
-                            state.at[:, band, window(row, count), :],
-                            state.at[:, band, window(row + by, count), :],
-                            row_send.at[side],
-                            row_recv.at[side],
-                            to_x,
-                        ).start()
-
-        each_plane(pass_on)
+
+                @pl.when(there)
+                def _(side=side, by=by, to_x=to_x):
+                    row_copy(
+                        state.at[:, band, window(row, count), :],
+                        state.at[:, band, window(row + by, count), :],
+                        row_send.at[side],
+                        row_recv.at[side],
+                        to_x,
+                    ).start()
+
+        if part in DIRECT:
+            tiles_of(row, count, MEMBERS - 1)(deliver_recv.at[part, 0])
+        else:
+            each_plane(pass_on)
 
     passed = [
         sum(

time: 32 us -> 32 us (level)
  no operation moved by 1% of the time
where the time goes in v8:
time: 32 us; the launch traced here: 31.5 us
  Pallas kernels  30.8 us (96%)
  local copies, waits for them, and re-layouts  0.71 us (2%)
    pallas_call x1, Pallas kernels, per_device(): pl.pallas_call(kernel, out_shape=pltpu.VMEM(ensemble.shape, F32), in_spec...  30.8 us
    unnamed x1, local copies, waits for them, and re-layouts  0.71 us

profile of v8, /device:TPU:1, one launch (start us, length us, event | category | flops | bytes accessed | tf_op | source)
XLA Modules:
  0.0 31.5 jit_solution(9351235090768705042)
XLA Ops:
  0.0 30.8 %filter_step.1 = f32[1,2,8,4096]{3,2,1,0:T(8,128)S(1)} custom-call(s32[64]{0:T(128)} %offspring_in.1, s32[64]{0:T(128)} %new_owner_in.1, f32[8]{0:T(128)} %nudge_in.1, f32[1,2,8,4096]{3,2,1,0:T(8,128)} %ensemble.1, bf16[1,2,2,8,4096]{4,3,2,1,0:T(8,128)(2,1)} %perturb.1, f32[8,4096]{1,0:T(8,128)} %observed.1), custom_call_target="tpu_custom_call" | custom-call | tf_op jit(solution)/shard_map/filter_step/pallas_call | solution.py:406
  30.8 0.7 %copy.8 = f32[1,2,8,4096]{3,2,1,0:T(8,128)} copy(f32[1,2,8,4096]{3,2,1,0:T(8,128)S(1)} %filter_step.1) | data formatting | bytes 524288

commit v9 on v8

--- a/solution.py
+++ b/solution.py
@@ -17,10 +17,10 @@
 BAND = TILES // PLANES
 SPAN = 3 * ROWS
 HALO = 6
-SPREAD = ((2, 2), (4, 2), (0, 2), (6, 2))
-DELIVER = (((2, 2),), ((4, 2),), ((0, 2),), ((6, 2),))
+SPREAD = ((2, 2), (4, 2), (1, 1), (6, 1), (0, 1), (7, 1))
+DELIVER = tuple((p,) for p in SPREAD)
 PARTS = [(spread, *rows) for spread, parts in enumerate(DELIVER) for rows in parts]
-DIRECT = (2, 3)
+DIRECT = (4, 5)
 COUPLE = (0.4, 0.6)
 DRAG = (0.0, 0.2)
 DT = 0.05
@@ -256,15 +256,6 @@
             for place in range(PER_PLANE):
                 m = z * PER_PLANE + place
                 picked[part][m, rows] = tiles[spread][parent_at[0, m], rows]
-            for at_y, at_core in places[:count]:
-                to = z * PER_PLANE + at_y * 2 + at_core
-                pltpu.make_async_remote_copy(
-                    src_ref=picked[part].at[to, rows],
-                    dst_ref=state.at[core, my_tile, lands, :],
-                    send_sem=deliver_send.at[part],
-                    recv_sem=deliver_recv.at[part, 0 if part in DIRECT else plane],
-                    device_id=(to, x),
-                ).start()
             if part in DIRECT:
                 for side, (by, to_x, there) in sides_of(row):
 
@@ -279,6 +270,15 @@
                                 recv_sem=direct_recv.at[part],
                                 device_id=(to, to_x),
                             ).start()
+            for at_y, at_core in places[:count]:
+                to = z * PER_PLANE + at_y * 2 + at_core
+                pltpu.make_async_remote_copy(
+                    src_ref=picked[part].at[to, rows],
+                    dst_ref=state.at[core, my_tile, lands, :],
+                    send_sem=deliver_send.at[part],
+                    recv_sem=deliver_recv.at[part, 0 if part in DIRECT else plane],
+                    device_id=(to, x),
+                ).start()
 
         each_plane(deliver_in)
         state[core, my_tile, lands, :] = picked[part][me, rows]

time: 32 us -> 32 us (level); the launches traced: 31.5 us -> 31.9 us
  Pallas kernels: 30.8 us -> 31.2 us
    pallas_call x1, Pallas kernels: 30.8 us -> 31.2 us  [per_device(): pl.pallas_call(kernel, out_shape=pltpu.VMEM(ensemble.shape, F32), in_spec...]
where the time goes in v9:
time: 32 us; the launch traced here: 31.9 us
  Pallas kernels  31.2 us (98%)
  local copies, waits for them, and re-layouts  0.71 us (2%)
    pallas_call x1, Pallas kernels, per_device(): pl.pallas_call(kernel, out_shape=pltpu.VMEM(ensemble.shape, F32), in_spec...  31.2 us
    unnamed x1, local copies, waits for them, and re-layouts  0.71 us

profile of v9, /device:TPU:1, one launch (start us, length us, event | category | flops | bytes accessed | tf_op | source)
XLA Modules:
  0.0 31.9 jit_solution(2287979017908540717)
XLA Ops:
  0.0 31.2 %filter_step.1 = f32[1,2,8,4096]{3,2,1,0:T(8,128)S(1)} custom-call(s32[64]{0:T(128)} %offspring_in.1, s32[64]{0:T(128)} %new_owner_in.1, f32[8]{0:T(128)} %nudge_in.1, f32[1,2,8,4096]{3,2,1,0:T(8,128)} %ensemble.1, bf16[1,2,2,8,4096]{4,3,2,1,0:T(8,128)(2,1)} %perturb.1, f32[8,4096]{1,0:T(8,128)} %observed.1), custom_call_target="tpu_custom_call" | custom-call | tf_op jit(solution)/shard_map/filter_step/pallas_call | solution.py:406
  31.2 0.7 %copy.8 = f32[1,2,8,4096]{3,2,1,0:T(8,128)} copy(f32[1,2,8,4096]{3,2,1,0:T(8,128)S(1)} %filter_step.1) | data formatting | bytes 524288
